TPU v7x, 256 devices: a whole 4x4x8 slice. The times are simulated.
256 devices in a mesh: dp: 8 (over x, core), latent: 32 (over z, y).
Axes of the slice: x: 4, y: 4, z: 8, core: 2. Of those that a mesh axis runs over, the one named last changes fastest.
Arguments:
- tokens: bfloat16 [4096, 8192], P('dp', 'latent'), may hold values from -6 to 6
- enc_weight: bfloat16 [8192, 8192], P('latent'), may hold values from -0.0625 to 0.0625
- dec_weight: bfloat16 [8192, 8192], P('latent'), may hold values from -0.1875 to 0.1875
- active_blocks: int32 [32, 8], P('dp'), may hold values from 0 to 63, all different within a row
- counts: int32 [4096], P('dp'), may hold values from 0 to 3
Outputs:
- grad_enc: float32 [8192, 8192], P('latent', 'dp')
- grad_dec: float32 [8192, 8192], P('latent', 'dp')
Inputs may be any that keep to these rules, and one draw needn't show every extreme that they name: `active_blocks`: each row lists 8 distinct latent blocks, and every latent block is listed in some row.
All inputs are finite; a program needn't handle non-finite values.
Results may differ from a plain program's by a relative error of at most 0.02.
Values may be sent and summed in bfloat16 or wider, within the bound.
No kernel may reach another device: no remote copies, remote signals or barrier semaphores. Data moves between devices by JAX's collectives and lax.ppermute only.
A program may use at most 128 MiB of HBM per device.

v0:
```python
import jax
import jax.numpy as jnp
from jax import lax
from jax.sharding import PartitionSpec as P

BLOCK = 128


def matmul_nt(left, right):
    return lax.dot_general(
        left, right, (((1,), (1,)), ((), ())), preferred_element_type=jnp.float32
    )


def matmul_tn(left, right):
    return lax.dot_general(
        left, right, (((0,), (0,)), ((), ())), preferred_element_type=jnp.float32
    )


def per_device(tokens, enc_weight, dec_weight, active_blocks, counts):
    lat_rows = enc_weight.shape[0]
    lb_local = lat_rows // BLOCK
    block_ids = lax.axis_index("latent") * lb_local + jnp.arange(lb_local, dtype=jnp.int32)
    hits = jnp.any(active_blocks[:, :, None] == block_ids[None, None, :], axis=1).astype(
        jnp.float32
    )
    mask = jnp.repeat(jnp.repeat(hits, BLOCK, axis=0), BLOCK, axis=1)
    whole = lax.all_gather(tokens, "latent", axis=1, tiled=True)
    pre = matmul_nt(whole, enc_weight)
    codes = (mask * pre).astype(jnp.bfloat16)
    partial_value = jnp.dot(codes, dec_weight, preferred_element_type=jnp.float32)
    weights = counts.astype(jnp.float32)[:, None] / BLOCK
    recon_share = lax.psum_scatter(
        partial_value.astype(jnp.bfloat16), "latent", scatter_dimension=1, tiled=True
    ).astype(jnp.float32)
    share_out = (weights * (recon_share - tokens.astype(jnp.float32))).astype(jnp.bfloat16)
    grad_out = lax.all_gather(share_out, "latent", axis=1, tiled=True)
    grad_codes = (mask * matmul_nt(grad_out, dec_weight)).astype(jnp.bfloat16)
    group_dec = matmul_tn(codes, grad_out).astype(jnp.bfloat16)
    group_enc = matmul_tn(grad_codes, whole).astype(jnp.bfloat16)
    grad_dec, grad_enc = (
        lax.psum_scatter(group_dec, "dp", scatter_dimension=1, tiled=True).astype(jnp.float32),
        lax.psum_scatter(group_enc, "dp", scatter_dimension=1, tiled=True).astype(jnp.float32),
    )
    return (grad_enc, grad_dec)


def solution(mesh):
    return jax.shard_map(
        per_device,
        mesh=mesh,
        in_specs=(P("dp", "latent"), P("latent", None), P("latent", None), P("dp", None), P("dp")),
        out_specs=(P("latent", "dp"), P("latent", "dp")),
        check_vma=False,
    )
```

profile of v0, /device:TPU:2, one launch (start us, length us, event | category | flops | bytes accessed | tf_op | source)
XLA Modules:
  0.0 567.0 jit_solution(7569797376845332983)
XLA Ops:
  7.2 0.0 all-gather.3.cloned.1.call-start
  7.2 0.7 all-gather.3.cloned.1.call-update
  7.9 0.0 reduce-scatter.4.cloned.1.call-start
  8.0 0.9 compare_reduce_fusion
  8.9 0.1 copy.7
  9.0 108.2 %all-gather.3.cloned.1.call-done = bf16[512,8192]{1,0:T(8,128)(2,1)} async-done(((bf16[512,256]{1,0:T(8,128)(2,1)}), bf16[512,8192]{1,0:T(8,128)(2,1)}) %all-gather.3.cloned.1.call-update) | async-done | bytes 8388624 | tf_op jit(solution)/shard_map/all_gather | solution.py:29
  117.1 0.0 copy-start
  117.2 0.6 broadcast_in_dim.10
  117.8 7.2 %fusion = bf16[512,256]{1,0:T(8,128)(2,1)S(1)} fusion(bf16[512,8192]{1,0:T(8,128)(2,1)} %all-gather.3.cloned.1.call-done, bf16[256,8192]{1,0:T(8,128)(2,1)} %param.6, f32[64,8,2,128]{3,2,1,0:T(2,128)S(1)} %bitcast.27), kind=kOutput, calls=%fused_computation.5 | convolution fusion | flops 2147745792 | bytes 13369344 | tf_op jit(solution)/shard_map/dot_general | solution.py:10
  125.0 0.0 copy-done
  125.0 0.0 copy-start.2
  125.0 0.0 copy-start.1
  125.0 5.6 convolution_convert_fusion
  130.6 0.0 reduce-scatter.4.cloned.1.call-update
  130.6 0.0 all-gather.5.cloned.1.call-start
  130.7 0.0 copy-done.2
  130.7 227.6 %reduce-scatter.4.cloned.1.call-done = bf16[512,256]{1,0:T(8,128)(2,1)} async-done(((bf16[512,8192]{1,0:T(8,128)(2,1)}), bf16[512,256]{1,0:T(8,128)(2,1)}) %reduce-scatter.4.cloned.1.call-update) | async-done | bytes 262160 | tf_op jit(solution)/shard_map/reduce_scatter | solution.py:34
  358.4 0.0 copy-done.1
  358.4 1.8 multiply_convert_fusion
  360.1 0.0 all-gather.5.cloned.1.call-update
  360.2 0.2 reduce-scatter.6.cloned.1.call-start
  360.4 103.5 %all-gather.5.cloned.1.call-done = bf16[512,8192]{1,0:T(8,128)(2,1)} async-done(((bf16[512,256]{1,0:T(8,128)(2,1)}), bf16[512,8192]{1,0:T(8,128)(2,1)}) %all-gather.5.cloned.1.call-update) | async-done | bytes 8388624 | tf_op jit(solution)/shard_map/all_gather | solution.py:38
  463.9 17.9 %convolution_convert_fusion.2 = bf16[256,8192]{1,0:T(8,128)(2,1)} fusion(bf16[512,8192]{1,0:T(8,128)(2,1)} %all-gather.3.cloned.1.call-done, bf16[512,8192]{1,0:T(8,128)(2,1)} %all-gather.5.cloned.1.call-done, bf16[256,8192]{1,0:T(8,128)(2,1)} %param.7, f32[64,8,2,128]{3,2,1,0:T(2,128)S(1)} %bitcast.28), kind=kOutput, calls=%fused_computation.2 | convolution fusion | flops 4297326592 | bytes 25690112 | tf_op jit(solution)/shard_map/dot_general | solution.py:16
  481.8 0.0 reduce-scatter.6.cloned.1.call-update
  481.8 0.0 reduce-scatter.8.cloned.1.call-start
  481.9 7.7 %convolution_convert_fusion.1 = bf16[256,8192]{1,0:T(8,128)(2,1)} fusion(bf16[512,256]{1,0:T(8,128)(2,1)S(1)} %fusion, bf16[512,8192]{1,0:T(8,128)(2,1)} %all-gather.5.cloned.1.call-done), kind=kOutput, calls=%fused_computation.1 | convolution fusion | flops 2149580800 | bytes 12845056 | tf_op jit(solution)/shard_map/dot_general | solution.py:16
  489.6 0.0 reduce-scatter.8.cloned.1.call-update
  489.6 26.8 %reduce-scatter.6.cloned.1.call-done = bf16[256,1024]{1,0:T(8,128)(2,1)} async-done(((bf16[256,8192]{1,0:T(8,128)(2,1)}), bf16[256,1024]{1,0:T(8,128)(2,1)}) %reduce-scatter.6.cloned.1.call-update) | async-done | bytes 524304 | tf_op jit(solution)/shard_map/reduce_scatter | solution.py:44
  516.4 2.1 convert_element_type.45
  518.5 39.9 %reduce-scatter.8.cloned.1.call-done = bf16[256,1024]{1,0:T(8,128)(2,1)} async-done(((bf16[256,8192]{1,0:T(8,128)(2,1)}), bf16[256,1024]{1,0:T(8,128)(2,1)}) %reduce-scatter.8.cloned.1.call-update) | async-done | bytes 524304 | tf_op jit(solution)/shard_map/reduce_scatter | solution.py:43
  558.4 2.1 convert_element_type.47
  (4 shorter events, 0.0 us)
Async XLA Ops:
  7.2 110.0 %all-gather.3.cloned.1.call-start = ((), (), s32[]{:S(2)}) async-start(), calls=%async_computation.3 | async-start | bytes 8650752 | tf_op jit(solution)/shard_map/all_gather | solution.py:29
  7.9 350.5 %reduce-scatter.4.cloned.1.call-start = ((), (), s32[]{:S(2)}) async-start(), calls=%async_computation.4 | async-start | bytes 8650752 | tf_op jit(solution)/shard_map/reduce_scatter | solution.py:34
  117.1 7.9 %copy-start = (bf16[256,8192]{1,0:T(8,128)(2,1)S(1)}, bf16[256,8192]{1,0:T(8,128)(2,1)}, u32[]{:S(2)}) copy-start(bf16[256,8192]{1,0:T(8,128)(2,1)} %param.7) | copy-start | bytes 12582916
  125.0 5.7 %copy-start.2 = (s32[512]{0:T(512)S(1)}, s32[512]{0:T(512)}, u32[]{:S(2)}) copy-start(s32[512]{0:T(512)} %param.9) | copy-start | bytes 6148
  125.0 233.3 %copy-start.1 = (bf16[512,256]{1,0:T(8,128)(2,1)S(1)}, bf16[512,256]{1,0:T(8,128)(2,1)}, u32[]{:S(2)}) copy-start(bf16[512,256]{1,0:T(8,128)(2,1)} %param.5) | copy-start | bytes 786436
  130.6 333.2 %all-gather.5.cloned.1.call-start = ((), (), s32[]{:S(2)}) async-start(), calls=%async_computation.5 | async-start | bytes 8650752 | tf_op jit(solution)/shard_map/all_gather | solution.py:38
  360.2 156.2 %reduce-scatter.6.cloned.1.call-start = ((), (), s32[]{:S(2)}) async-start(), calls=%async_computation.6 | async-start | bytes 4718592 | tf_op jit(solution)/shard_map/reduce_scatter | solution.py:44
  481.8 76.5 %reduce-scatter.8.cloned.1.call-start = ((), (), s32[]{:S(2)}) async-start(), calls=%async_computation.7 | async-start | bytes 4718592 | tf_op jit(solution)/shard_map/reduce_scatter | solution.py:43
Sparse Core Ops, SparseCore 0:
  10.5 106.6 all-gather.2
  130.8 227.5 reduce-scatter.3
  361.7 102.1 all-gather.4
  482.0 34.3 reduce-scatter.5
  518.9 39.3 reduce-scatter.7
where the time goes:
time: 571 us; the launch traced here: 567 us
  waiting for transfers between devices  507 us (89%)
  matrix products  38.5 us (7%)
  between operations  13.9 us (2%)
  other arithmetic  6.95 us (1%)
    reduce_scatter x1, waiting for transfers between devices, per_device(): lax.psum_scatter(partial_value.astype(jnp.bfloat16), 'latent', scatter_di...  228 us
    all_gather x1, waiting for transfers between devices, per_device(): whole = lax.all_gather(tokens, 'latent', axis=1, tiled=True)  108 us
    all_gather x1, waiting for transfers between devices, per_device(): grad_out = lax.all_gather(share_out, 'latent', axis=1, tiled=True)  103 us
    reduce_scatter x1, waiting for transfers between devices, per_device(): lax.psum_scatter(group_dec, 'dp', scatter_dimension=1, tiled=True)  39.9 us
    reduce_scatter x1, waiting for transfers between devices, per_device(): lax.psum_scatter(group_enc, 'dp', scatter_dimension=1, tiled=True)  26.8 us
    dot_general x2, matrix products, matmul_tn(): lax.dot_general(left, right, (((0,), (0,)), ((), ())), preferred_element_...  25.6 us
  transfers between devices with their start and end apart: 5, of which 5 were waited for; matrix products, arithmetic and copies ran while one was open for 2% of the time, Pallas kernels for 0%

commit v1 on v0

v1 whole, which is shorter than its diff:
```python
import functools

import jax
import jax.numpy as jnp
import numpy as np
from jax import lax
from jax.experimental import pallas as pl
from jax.experimental.pallas import tpu as pltpu
from jax.sharding import Mesh
from jax.sharding import PartitionSpec as P

BLOCK = 128
VMEM = pltpu.CompilerParams(vmem_limit_bytes=48 * 1024 * 1024)
NT = (((1,), (1,)), ((), ()))
TN = (((0,), (0,)), ((), ()))
SMEM_SPEC = pl.BlockSpec(memory_space=pltpu.SMEM)
VMEM_SPEC = pl.BlockSpec(memory_space=pltpu.VMEM)


def dot(left, right, dims):
    return lax.dot_general(left, right, dims, preferred_element_type=jnp.float32)


def pre_kernel(tb, act, ids_ref, tok_ref, enc_ref, out_ref):
    for t in range(tb):
        rows = tok_ref[t * BLOCK : (t + 1) * BLOCK, :]
        for a in range(act):
            out_ref[t * act + a] = dot(rows, enc_ref[ids_ref[t, a]], NT).astype(jnp.bfloat16)


def sum_rows(tb, act, ids_ref, codes_ref, rows_of, acc_ref, out_ref):
    acc_ref[...] = jnp.zeros_like(acc_ref)
    for t in range(tb):
        rows = rows_of(t)
        for a in range(act):
            acc_ref[ids_ref[t, a]] += dot(codes_ref[t * act + a], rows, TN)

    @pl.loop(0, acc_ref.shape[0])
    def _(b):
        out_ref[b] = acc_ref[b].astype(jnp.bfloat16)


def dec_kernel(tb, act, ids_ref, tok_ref, weight_ref, codes_ref, dec_ref, part_ref, grad_ref, acc_ref, gout_ref):
    for t in range(tb):
        here = slice(t * BLOCK, (t + 1) * BLOCK)
        recon = jnp.zeros((BLOCK, tok_ref.shape[1]), jnp.float32)
        for a in range(act):
            recon += jnp.dot(codes_ref[t * act + a], dec_ref[ids_ref[t, a]], preferred_element_type=jnp.float32)
        gout = (weight_ref[here, :] * (recon - tok_ref[here, :].astype(jnp.float32))).astype(jnp.bfloat16)
        gout_ref[here, :] = gout
        for a in range(act):
            part_ref[t * act + a] = dot(gout, dec_ref[ids_ref[t, a]], NT).astype(jnp.bfloat16)
    sum_rows(tb, act, ids_ref, codes_ref, lambda t: gout_ref[t * BLOCK : (t + 1) * BLOCK, :], acc_ref, grad_ref)


def enc_kernel(tb, act, ids_ref, tok_ref, codes_ref, grad_ref, acc_ref):
    sum_rows(tb, act, ids_ref, codes_ref, lambda t: tok_ref[t * BLOCK : (t + 1) * BLOCK, :], acc_ref, grad_ref)


def all_sum(part, axes, n):
    got = lax.all_to_all(part, axes, 0, 0, tiled=True)
    mine = jnp.sum(got.astype(jnp.float32), axis=0).astype(part.dtype)
    return lax.all_to_all(jnp.broadcast_to(mine[None], part.shape), axes, 0, 0, tiled=True)


def per_device(tokens, enc_weight, dec_weight, active_blocks, counts, *, sizes):
    nx, nc, nz, ny = (sizes[k] for k in ("x", "c", "z", "y"))
    nd = nx * nc
    feats = ("x", "c", "y")
    tok_dev, width = tokens.shape
    tb, act = active_blocks.shape
    rows = enc_weight.shape[0]
    lat_blocks = rows * nz * ny // BLOCK
    d = lax.axis_index(("x", "c"))

    swap = [(g * nz + z, z * nz + g) for g in range(nd) for z in range(nz)]
    tok = lax.ppermute(tokens, ("x", "c", "z"), swap)
    small = jnp.concatenate([counts, active_blocks.reshape(-1)])
    small = lax.ppermute(small, ("x", "c", "z"), swap)
    weights = small[:tok_dev].astype(jnp.float32)[:, None] / BLOCK
    ids = small[tok_dev:].reshape(tb, act)

    def all_rows(weight):
        mine = lax.dynamic_slice_in_dim(weight, d * (ny * width), ny * width, axis=1)
        mine = mine.reshape(rows, ny, width).transpose(1, 0, 2)
        mine = lax.all_to_all(mine, "y", 0, 0, tiled=True).reshape(ny * rows, width)
        whole = lax.all_gather(mine, "z", axis=0, tiled=True)
        return whole.reshape(lat_blocks, BLOCK, width)

    def own_rows(grad):
        part = lax.psum_scatter(grad.reshape(nz * ny * rows, width), "z", scatter_dimension=0, tiled=True)
        part = lax.all_to_all(part.reshape(ny, rows, width), "y", 0, 0, tiled=True)
        return part.transpose(1, 0, 2).reshape(rows, ny * width).astype(jnp.float32)

    enc = all_rows(enc_weight)
    dec = all_rows(dec_weight)

    pairs = jax.ShapeDtypeStruct((tb * act, BLOCK, BLOCK), jnp.bfloat16)
    grads = jax.ShapeDtypeStruct((lat_blocks, BLOCK, width), jnp.bfloat16)
    acc = pltpu.VMEM((lat_blocks, BLOCK, width), jnp.float32)

    part = pl.pallas_call(
        functools.partial(pre_kernel, tb, act),
        out_shape=pairs,
        in_specs=[SMEM_SPEC, VMEM_SPEC, VMEM_SPEC],
        out_specs=VMEM_SPEC,
        compiler_params=VMEM,
    )(ids, tok, enc)
    codes = all_sum(part, feats, nd * ny)
    part, group_dec = pl.pallas_call(
        functools.partial(dec_kernel, tb, act),
        out_shape=(pairs, grads),
        in_specs=[SMEM_SPEC] + [VMEM_SPEC] * 4,
        out_specs=(VMEM_SPEC, VMEM_SPEC),
        scratch_shapes=[acc, pltpu.VMEM((tok_dev, width), jnp.bfloat16)],
        compiler_params=VMEM,
    )(ids, tok, weights, codes, dec)
    grad_dec = own_rows(group_dec)
    grad_codes = all_sum(part, feats, nd * ny)
    group_enc = pl.pallas_call(
        functools.partial(enc_kernel, tb, act),
        out_shape=grads,
        in_specs=[SMEM_SPEC] + [VMEM_SPEC] * 2,
        out_specs=VMEM_SPEC,
        scratch_shapes=[acc],
        compiler_params=VMEM,
    )(ids, tok, grad_codes)
    grad_enc = own_rows(group_enc)
    return (grad_enc, grad_dec)


def solution(mesh):
    fine = Mesh(np.asarray(mesh.devices).reshape(4, 2, 8, 4), ("x", "c", "z", "y"))
    dp, latent = ("x", "c"), ("z", "y")
    return jax.shard_map(
        functools.partial(per_device, sizes=dict(fine.shape)),
        mesh=fine,
        in_specs=(P(dp, latent), P(latent, None), P(latent, None), P(dp, None), P(dp)),
        out_specs=(P(latent, dp), P(latent, dp)),
        check_vma=False,
    )
```

time: 571 us -> 293 us (0.51)
  waiting for transfers between devices: 507 us -> 130 us
  blocking collectives: 0 us -> 106 us
  matrix products: 38.5 us -> 0 us
  starting transfers between devices: 0.38 us -> 17.3 us
  local copies, waits for them, and re-layouts: 0.73 us -> 12.6 us
  Pallas kernels: 0 us -> 11.3 us
  other arithmetic: 6.95 us -> 0.49 us
    reduce_scatter x3 -> x2, waiting for transfers between devices: 294 us -> 48.1 us  [own_rows(): lax.psum_scatter(grad.reshape(nz * ny * rows, width), 'z', scatter_dimens...]
    all_gather x2, waiting for transfers between devices: 212 us -> 52.5 us  [all_rows(): whole = lax.all_gather(mine, 'z', axis=0, tiled=True)]
    all_to_all x0 -> x6, blocking collectives: none -> 106 us  [the longest x2 47.2 us: all_sum(): got = lax.all_to_all(part, axes, 0, 0, tiled=True)]
    dot_general x4 -> x0, matrix products: 38.5 us -> none  [the longest x2 25.6 us: matmul_tn(): lax.dot_general(left, right, (((0,), (0,)), ((), ())), preferred_element_...]
    ppermute x0 -> x2, waiting for transfers between devices: none -> 21.6 us  [the longest x1 21.6 us: per_device(): small = lax.ppermute(small, ('x', 'c', 'z'), swap)]
    pallas_call x0 -> x3, Pallas kernels: none -> 11.3 us  [the longest x1 7.59 us: per_device(): pl.pallas_call(functools.partial(dec_kernel, tb, act), out_shape=(pairs,...]
    all_to_all x0 -> x2, starting transfers between devices: none -> 9.51 us  [the longest x1 5.22 us: all_sum(): lax.all_to_all(jnp.broadcast_to(mine[None], part.shape), axes, 0, 0, tile...]
    all_to_all x0 -> x2, waiting for transfers between devices: none -> 7.92 us  [the longest x1 7.92 us: own_rows(): part = lax.all_to_all(part.reshape(ny, rows, width), 'y', 0, 0, tiled=True)]
  transfers between devices with their start and end apart: 5 -> 8, of which waited for: 5 -> 6; matrix products, arithmetic and copies ran while one was open for 2% -> 2% of each run, Pallas kernels for 0% -> 1%
where the time goes in v1:
time: 293 us; the launch traced here: 292 us
  waiting for transfers between devices  130 us (44%)
  blocking collectives  106 us (36%)
  starting transfers between devices  17.3 us (6%)
  between operations  13.9 us (5%)
  local copies, waits for them, and re-layouts  12.6 us (4%)
  Pallas kernels  11.3 us (4%)
    all_gather x2, waiting for transfers between devices, all_rows(): whole = lax.all_gather(mine, 'z', axis=0, tiled=True)  52.5 us
    reduce_scatter x2, waiting for transfers between devices, own_rows(): lax.psum_scatter(grad.reshape(nz * ny * rows, width), 'z', scatter_dimens...  48.1 us
    all_to_all x2, blocking collectives, all_sum(): got = lax.all_to_all(part, axes, 0, 0, tiled=True)  47.2 us
    all_to_all x2, blocking collectives, all_rows(): mine = lax.all_to_all(mine, 'y', 0, 0, tiled=True).reshape(ny * rows, width)  24.7 us
    ppermute x1, waiting for transfers between devices, per_device(): small = lax.ppermute(small, ('x', 'c', 'z'), swap)  21.6 us
    all_to_all x1, blocking collectives, all_sum(): lax.all_to_all(jnp.broadcast_to(mine[None], part.shape), axes, 0, 0, tile...  20.7 us
    all_to_all x1, blocking collectives, own_rows(): part = lax.all_to_all(part.reshape(ny, rows, width), 'y', 0, 0, tiled=True)  13.8 us
    all_to_all x1, waiting for transfers between devices, own_rows(): part = lax.all_to_all(part.reshape(ny, rows, width), 'y', 0, 0, tiled=True)  7.92 us
  transfers between devices with their start and end apart: 8, of which 6 were waited for; matrix products, arithmetic and copies ran while one was open for 2% of the time, Pallas kernels for 1%

profile of v1, /device:TPU:2, one launch (start us, length us, event | category | flops | bytes accessed | tf_op | source)
XLA Modules:
  0.0 292.2 jit_solution(10589198983903948288)
XLA Ops:
  7.2 0.0 all-gather.3.cloned.1.call-start
  7.2 1.3 constant_dynamic-slice_fusion
  8.5 0.0 copy-start.4
  8.5 0.2 copy.35
  8.7 13.7 %all_to_all.40 = bf16[4,256,256]{1,2,0:T(8,128)(2,1)S(1)} all-to-all(bf16[4,256,256]{1,2,0:T(8,128)(2,1)S(1)} %bitcast.29), channel_id=1, replica_groups=mesh['x'=4,'c'=2,'z'=8,'y'=4] {'y'}, dimensions={0} | all-to-all | bytes 1048576 | tf_op jit(solution)/shard_map/all_to_all | solution.py:86
  22.5 1.0 copy.27
  23.5 0.0 all-gather.3.cloned.1.call-update
  23.5 0.0 all-gather.5.cloned.1.call-start
  23.6 0.2 copy.36
  23.8 11.0 %all_to_all.41 = bf16[4,256,256]{1,2,0:T(8,128)(2,1)S(1)} all-to-all(bf16[4,256,256]{1,2,0:T(8,128)(2,1)S(1)} %bitcast.30), channel_id=1, replica_groups=mesh['x'=4,'c'=2,'z'=8,'y'=4] {'y'}, dimensions={0} | all-to-all | bytes 1048576 | tf_op jit(solution)/shard_map/all_to_all | solution.py:86
  34.7 1.0 copy.29
  35.7 0.0 all-gather.5.cloned.1.call-update
  35.8 5.2 %collective-permute-start.1 = (bf16[512,256]{1,0:T(8,128)(2,1)S(1)}, bf16[512,256]{1,0:T(8,128)(2,1)S(1)}, u32[]{:S(2)}, u32[]{:S(2)}) collective-permute-start(bf16[512,256]{1,0:T(8,128)(2,1)S(1)} %copy-done.4), channel_id=1, source_target_pairs={{0,0},{4,32},{8,64},{12,96},{16,128},{20,160},{24,192},{28,224},{3... | collective-permute-start | bytes 786440 | tf_op jit(solution)/shard_map/ppermute | solution.py:77
  40.9 0.1 reshape.57
  41.0 2.5 collective-permute-start
  43.5 21.6 %collective-permute-done = s32[544]{0:T(1024)S(1)} collective-permute-done((s32[544]{0:T(1024)S(1)}, s32[544]{0:T(1024)S(1)}, u32[]{:S(2)}, u32[]{:S(2)}) %collective-permute-start) | collective-permute-done | bytes 2208 | tf_op jit(solution)/shard_map/ppermute | solution.py:79
  65.1 0.1 reshape.58.ids_ref
  65.2 27.7 %all-gather.3.cloned.1.call-done = bf16[8192,256]{1,0:T(8,128)(2,1)} async-done(((bf16[1024,256]{1,0:T(8,128)(2,1)}), bf16[8192,256]{1,0:T(8,128)(2,1)}) %all-gather.3.cloned.1.call-update) | async-done | bytes 4194320 | tf_op jit(solution)/shard_map/all_gather | solution.py:87
  92.9 2.2 copy-done.1
  95.1 1.3 shard_map.68
  96.3 24.2 %all_to_all.42 = bf16[32,128,128]{2,1,0:T(8,128)(2,1)S(1)} all-to-all(bf16[32,128,128]{2,1,0:T(8,128)(2,1)S(1)} %shard_map.68), channel_id=1, replica_groups=mesh['x'=4,'c'=2,'z'=8,'y'=4] {'x','c','y'}, dimensions={0} | all-to-all | bytes 2097152 | tf_op jit(solution)/shard_map/all_to_all | solution.py:61
  120.6 0.2 reduce_sum.24
  120.7 1.2 broadcast_in_dim.4
  121.9 5.2 %all-to-all-start.2 = ((bf16[32,128,128]{2,1,0:T(8,128)(2,1)}), bf16[32,128,128]{2,1,0:T(8,128)(2,1)S(1)}, u32[]{:S(2)}, u32[]{:S(2)}) async-start(bf16[32,128,128]{2,1,0:T(8,128)(2,1)} %broadcast_in_dim.4), calls=%async_computation.2 | async-start | bytes 2097152 | tf_op jit(solution)/shard_map/all_to_all | solution.py:63
  127.2 0.0 reduce-scatter.5.cloned.1.call-start
  127.2 0.1 copy.30.weight_ref
  127.4 24.8 %all-gather.5.cloned.1.call-done = bf16[8192,256]{1,0:T(8,128)(2,1)} async-done(((bf16[1024,256]{1,0:T(8,128)(2,1)}), bf16[8192,256]{1,0:T(8,128)(2,1)}) %all-gather.5.cloned.1.call-update) | async-done | bytes 4194320 | tf_op jit(solution)/shard_map/all_gather | solution.py:87
  152.2 7.6 %shard_map.69 = (bf16[32,128,128]{2,1,0:T(8,128)(2,1)S(1)}, bf16[64,128,256]{2,1,0:T(8,128)(2,1)}) custom-call(s32[4,8]{1,0:T(4,128)S(1)} %reshape.58.ids_ref, bf16[512,256]{1,0:T(8,128)(2,1)S(1)} %collective-permute-done.1.tok_ref, f32[512,1]{1,0:T(8,128)S(1)} %copy.30.weight_ref, bf16[32,128,128]{2,1,0:T(8,128)(2,1)S(1)} %all-to-all-done.2.codes_ref, ...), custom_call_target="tpu_custom_call" | custom-call | tf_op jit(solution)/shard_map/pallas_call | solution.py:110
  159.8 0.0 reduce-scatter.5.cloned.1.call-update
  159.8 0.0 reduce-scatter.3.cloned.1.call-start
  159.8 23.0 %all_to_all.43 = bf16[32,128,128]{2,1,0:T(8,128)(2,1)S(1)} all-to-all(bf16[32,128,128]{2,1,0:T(8,128)(2,1)S(1)} %get-tuple-element.4), channel_id=1, replica_groups=mesh['x'=4,'c'=2,'z'=8,'y'=4] {'x','c','y'}, dimensions={0} | all-to-all | bytes 2097152 | tf_op jit(solution)/shard_map/all_to_all | solution.py:61
  182.8 0.2 reduce_sum.25
  183.0 0.2 broadcast_in_dim.5
  183.2 20.7 %all_to_all.44.codes_ref = bf16[32,128,128]{2,1,0:T(8,128)(2,1)S(1)} all-to-all(bf16[32,128,128]{2,1,0:T(8,128)(2,1)S(1)} %broadcast_in_dim.5), channel_id=1, replica_groups=mesh['x'=4,'c'=2,'z'=8,'y'=4] {'x','c','y'}, dimensions={0} | all-to-all | bytes 2097152 | tf_op jit(solution)/shard_map/all_to_all | solution.py:63
  203.9 2.4 shard_map.70
  206.3 2.0 copy-done
  208.3 0.0 reduce-scatter.3.cloned.1.call-update
  208.3 5.5 %reduce-scatter.5.cloned.1.call-done = bf16[1024,256]{1,0:T(8,128)(2,1)} async-done(((bf16[8192,256]{1,0:T(8,128)(2,1)}), bf16[1024,256]{1,0:T(8,128)(2,1)}) %reduce-scatter.5.cloned.1.call-update) | async-done | bytes 524304 | tf_op jit(solution)/shard_map/reduce_scatter | solution.py:91
  213.9 13.8 %all_to_all.45 = bf16[4,256,256]{2,1,0:T(8,128)(2,1)S(1)} all-to-all(bf16[4,256,256]{2,1,0:T(8,128)(2,1)} %bitcast.31), channel_id=1, replica_groups=mesh['x'=4,'c'=2,'z'=8,'y'=4] {'y'}, dimensions={0} | all-to-all | bytes 1048576 | tf_op jit(solution)/shard_map/all_to_all | solution.py:92
  227.7 42.6 %reduce-scatter.3.cloned.1.call-done = bf16[1024,256]{1,0:T(8,128)(2,1)} async-done(((bf16[8192,256]{1,0:T(8,128)(2,1)}), bf16[1024,256]{1,0:T(8,128)(2,1)}) %reduce-scatter.3.cloned.1.call-update) | async-done | bytes 524304 | tf_op jit(solution)/shard_map/reduce_scatter | solution.py:91
  270.2 4.3 %all-to-all-start.6 = ((bf16[4,256,256]{2,1,0:T(8,128)(2,1)}), bf16[4,256,256]{2,1,0:T(8,128)(2,1)S(1)}, u32[]{:S(2)}, u32[]{:S(2)}) async-start(bf16[4,256,256]{2,1,0:T(8,128)(2,1)} %bitcast.32), calls=%async_computation.7 | async-start | bytes 1048576 | tf_op jit(solution)/shard_map/all_to_all | solution.py:92
  274.5 0.2 copy.32
  274.7 0.1 convert_element_type.35
  274.8 1.3 copy.34
  276.1 7.9 %all-to-all-done.6 = bf16[4,256,256]{2,1,0:T(8,128)(2,1)S(1)} async-done(((bf16[4,256,256]{2,1,0:T(8,128)(2,1)}), bf16[4,256,256]{2,1,0:T(8,128)(2,1)S(1)}, u32[]{:S(2)}, u32[]{:S(2)}) %all-to-all-start.6) | async-done | bytes 524320 | tf_op jit(solution)/shard_map/all_to_all | solution.py:92
  284.0 0.2 copy.31
  284.2 0.1 convert_element_type.34
  284.3 1.3 copy.33
  (12 shorter events, 0.0 us)
Async XLA Ops:
  7.2 85.7 %all-gather.3.cloned.1.call-start = ((), (), s32[]{:S(2)}) async-start(), calls=%async_computation.10 | async-start | bytes 4718592 | tf_op jit(solution)/shard_map/all_gather | solution.py:87
  8.5 27.3 %copy-start.4 = (bf16[512,256]{1,0:T(8,128)(2,1)S(1)}, bf16[512,256]{1,0:T(8,128)(2,1)}, u32[]{:S(2)}) copy-start(bf16[512,256]{1,0:T(8,128)(2,1)} %param.5) | copy-start | bytes 786436
  8.5 32.4 %copy-start.2 = (s32[4,8]{1,0:T(4,128)S(1)}, s32[4,8]{1,0:T(4,128)}, u32[]{:S(2)}) copy-start(s32[4,8]{1,0:T(4,128)} %param.8) | copy-start | bytes 388
  8.5 32.5 %copy-start.3 = (s32[512]{0:T(512)S(1)}, s32[512]{0:T(512)}, u32[]{:S(2)}) copy-start(s32[512]{0:T(512)} %param.9) | copy-start | bytes 6148
  23.5 128.7 %all-gather.5.cloned.1.call-start = ((), (), s32[]{:S(2)}) async-start(), calls=%async_computation.11 | async-start | bytes 4718592 | tf_op jit(solution)/shard_map/all_gather | solution.py:87
  35.8 29.4 %collective-permute-start.1 = (bf16[512,256]{1,0:T(8,128)(2,1)S(1)}, bf16[512,256]{1,0:T(8,128)(2,1)S(1)}, u32[]{:S(2)}, u32[]{:S(2)}) collective-permute-start(bf16[512,256]{1,0:T(8,128)(2,1)S(1)} %copy-done.4), channel_id=1, source_target_pairs={{0,0},{4,32},{8,64},{12,96},{16,128},{20,160},{24,192},{28,224},{3... | collective-permute-start | bytes 786440 | tf_op jit(solution)/shard_map/ppermute | solution.py:77
  41.0 24.1 %collective-permute-start = (s32[544]{0:T(1024)S(1)}, s32[544]{0:T(1024)S(1)}, u32[]{:S(2)}, u32[]{:S(2)}) collective-permute-start(s32[544]{0:T(1024)S(1)} %pad_add_fusion), channel_id=1, source_target_pairs={{0,0},{4,32},{8,64},{12,96},{16,128},{20,160},{24,192},{28,224},{3... | collective-permute-start | bytes 6536 | tf_op jit(solution)/shard_map/ppermute | solution.py:79
  92.9 2.2 copy-start.1
  121.9 30.3 %all-to-all-start.2 = ((bf16[32,128,128]{2,1,0:T(8,128)(2,1)}), bf16[32,128,128]{2,1,0:T(8,128)(2,1)S(1)}, u32[]{:S(2)}, u32[]{:S(2)}) async-start(bf16[32,128,128]{2,1,0:T(8,128)(2,1)} %broadcast_in_dim.4), calls=%async_computation.2 | async-start | bytes 2097152 | tf_op jit(solution)/shard_map/all_to_all | solution.py:63
  127.2 86.7 %reduce-scatter.5.cloned.1.call-start = ((), (), s32[]{:S(2)}) async-start(), calls=%async_computation.13 | async-start | bytes 4718592 | tf_op jit(solution)/shard_map/reduce_scatter | solution.py:91
  159.8 110.4 %reduce-scatter.3.cloned.1.call-start = ((), (), s32[]{:S(2)}) async-start(), calls=%async_computation.12 | async-start | bytes 4718592 | tf_op jit(solution)/shard_map/reduce_scatter | solution.py:91
  206.3 2.0 copy-start
  270.2 13.8 %all-to-all-start.6 = ((bf16[4,256,256]{2,1,0:T(8,128)(2,1)}), bf16[4,256,256]{2,1,0:T(8,128)(2,1)S(1)}, u32[]{:S(2)}, u32[]{:S(2)}) async-start(bf16[4,256,256]{2,1,0:T(8,128)(2,1)} %bitcast.32), calls=%async_computation.7 | async-start | bytes 1048576 | tf_op jit(solution)/shard_map/all_to_all | solution.py:92
Sparse Core Ops, SparseCore 0:
  23.6 69.2 all-gather.2
  95.2 56.8 all-gather.4
  159.9 53.8 reduce-scatter.4
  216.3 53.9 reduce-scatter.2

commit v2 on v1

--- a/solution.py
+++ b/solution.py
@@ -77,13 +77,13 @@
     tok = lax.ppermute(tokens, ("x", "c", "z"), swap)
     small = jnp.concatenate([counts, active_blocks.reshape(-1)])
     small = lax.ppermute(small, ("x", "c", "z"), swap)
-    weights = small[:tok_dev].astype(jnp.float32)[:, None] / BLOCK
-    ids = small[tok_dev:].reshape(tb, act)
 
-    def all_rows(weight):
+    def own_features(weight):
         mine = lax.dynamic_slice_in_dim(weight, d * (ny * width), ny * width, axis=1)
         mine = mine.reshape(rows, ny, width).transpose(1, 0, 2)
-        mine = lax.all_to_all(mine, "y", 0, 0, tiled=True).reshape(ny * rows, width)
+        return lax.all_to_all(mine, "y", 0, 0, tiled=True).reshape(ny * rows, width)
+
+    def all_rows(mine):
         whole = lax.all_gather(mine, "z", axis=0, tiled=True)
         return whole.reshape(lat_blocks, BLOCK, width)
 
@@ -92,8 +92,11 @@
         part = lax.all_to_all(part.reshape(ny, rows, width), "y", 0, 0, tiled=True)
         return part.transpose(1, 0, 2).reshape(rows, ny * width).astype(jnp.float32)
 
-    enc = all_rows(enc_weight)
-    dec = all_rows(dec_weight)
+    mine, tok, small = lax.optimization_barrier((own_features(enc_weight), tok, small))
+    enc = all_rows(mine)
+    dec = all_rows(own_features(dec_weight))
+    weights = small[:tok_dev].astype(jnp.float32)[:, None] / BLOCK
+    ids = small[tok_dev:].reshape(tb, act)
 
     pairs = jax.ShapeDtypeStruct((tb * act, BLOCK, BLOCK), jnp.bfloat16)
     grads = jax.ShapeDtypeStruct((lat_blocks, BLOCK, width), jnp.bfloat16)

time: 293 us -> 292 us (level)
  blocking collectives: 106 us -> 92.9 us
  waiting for transfers between devices: 130 us -> 137 us
  starting transfers between devices: 17.3 us -> 21.7 us
    all_gather x2, waiting for transfers between devices: 52.5 us -> 65.6 us  [all_rows(): whole = lax.all_gather(mine, 'z', axis=0, tiled=True)]
    all_to_all x2 -> x1, blocking collectives: 24.7 us -> 12.5 us  [own_features(): return lax.all_to_all(mine, 'y', 0, 0, tiled=True).reshape(ny * rows, width)]
    ppermute x1, waiting for transfers between devices: 21.6 us -> 13.8 us  [per_device(): small = lax.ppermute(small, ('x', 'c', 'z'), swap)]
    all_to_all x0 -> x1, starting transfers between devices: none -> 4.46 us  [own_features(): return lax.all_to_all(mine, 'y', 0, 0, tiled=True).reshape(ny * rows, width)]
  transfers between devices with their start and end apart: 8 -> 9, of which waited for: 6 -> 7; matrix products, arithmetic and copies ran while one was open for 2% -> 2% of each run, Pallas kernels for 1% -> 1%
where the time goes in v2:
time: 292 us; the launch traced here: 291 us
  waiting for transfers between devices  137 us (47%)
  blocking collectives  92.9 us (32%)
  starting transfers between devices  21.7 us (7%)
  between operations  13.9 us (5%)
  local copies, waits for them, and re-layouts  13.4 us (5%)
  Pallas kernels  11.3 us (4%)
    all_gather x2, waiting for transfers between devices, all_rows(): whole = lax.all_gather(mine, 'z', axis=0, tiled=True)  65.6 us
    reduce_scatter x2, waiting for transfers between devices, own_rows(): lax.psum_scatter(grad.reshape(nz * ny * rows, width), 'z', scatter_dimens...  48.1 us
    all_to_all x2, blocking collectives, all_sum(): got = lax.all_to_all(part, axes, 0, 0, tiled=True)  46 us
    all_to_all x1, blocking collectives, all_sum(): lax.all_to_all(jnp.broadcast_to(mine[None], part.shape), axes, 0, 0, tile...  20.7 us
    all_to_all x1, blocking collectives, own_rows(): part = lax.all_to_all(part.reshape(ny, rows, width), 'y', 0, 0, tiled=True)  13.8 us
    ppermute x1, waiting for transfers between devices, per_device(): small = lax.ppermute(small, ('x', 'c', 'z'), swap)  13.8 us
    all_to_all x1, blocking collectives, own_features(): return lax.all_to_all(mine, 'y', 0, 0, tiled=True).reshape(ny * rows, width)  12.5 us
    unnamed x14, local copies, waits for them, and re-layouts  7.98 us
  transfers between devices with their start and end apart: 9, of which 7 were waited for; matrix products, arithmetic and copies ran while one was open for 2% of the time, Pallas kernels for 1%

profile of v2, /device:TPU:2, one launch (start us, length us, event | category | flops | bytes accessed | tf_op | source)
XLA Modules:
  0.0 290.9 jit_solution(14181823595004338682)
XLA Ops:
  7.2 1.3 constant_dynamic-slice_fusion
  8.5 1.0 copy.35
  9.5 4.5 %all-to-all-start = ((bf16[4,256,256]{1,2,0:T(8,128)(2,1)}), bf16[4,256,256]{1,2,0:T(8,128)(2,1)S(1)}, u32[]{:S(2)}, u32[]{:S(2)}) async-start(bf16[4,256,256]{1,2,0:T(8,128)(2,1)} %bitcast.1), calls=%async_computation | async-start | bytes 1048576 | tf_op jit(solution)/shard_map/all_to_all | solution.py:84
  14.0 5.1 %collective-permute-start = (bf16[512,256]{1,0:T(8,128)(2,1)S(1)}, bf16[512,256]{1,0:T(8,128)(2,1)S(1)}, u32[]{:S(2)}, u32[]{:S(2)}) collective-permute-start(bf16[512,256]{1,0:T(8,128)(2,1)S(1)} %copy-done.4), channel_id=1, source_target_pairs={{0,0},{4,32},{8,64},{12,96},{16,128},{20,160},{24,192},{28,224},{3... | collective-permute-start | bytes 786440 | tf_op jit(solution)/shard_map/ppermute | solution.py:77
  19.1 0.1 reshape.59
  19.2 2.5 collective-permute-start.1
  21.7 1.7 all-to-all-done
  23.5 1.0 copy.27
  24.5 13.8 %collective-permute-done.1 = s32[544]{0:T(1024)S(1)} collective-permute-done((s32[544]{0:T(1024)S(1)}, s32[544]{0:T(1024)S(1)}, u32[]{:S(2)}, u32[]{:S(2)}) %collective-permute-start.1) | collective-permute-done | bytes 2208 | tf_op jit(solution)/shard_map/ppermute | solution.py:79
  38.2 0.0 collective-permute-done.tok_ref
  38.2 0.0 all-gather.3.cloned.1.call-update
  38.3 0.0 all-gather.5.cloned.1.call-start
  38.3 0.2 copy.36
  38.5 12.5 %all_to_all.40 = bf16[4,256,256]{1,2,0:T(8,128)(2,1)S(1)} all-to-all(bf16[4,256,256]{1,2,0:T(8,128)(2,1)S(1)} %bitcast.29), channel_id=1, replica_groups=mesh['x'=4,'c'=2,'z'=8,'y'=4] {'y'}, dimensions={0} | all-to-all | bytes 1048576 | tf_op jit(solution)/shard_map/all_to_all | solution.py:84
  51.0 1.0 copy.29
  52.0 0.0 all-gather.5.cloned.1.call-update
  52.0 0.1 reshape.60.ids_ref
  52.1 43.0 %all-gather.3.cloned.1.call-done = bf16[8192,256]{1,0:T(8,128)(2,1)} async-done(((bf16[1024,256]{1,0:T(8,128)(2,1)}), bf16[8192,256]{1,0:T(8,128)(2,1)}) %all-gather.3.cloned.1.call-update) | async-done | bytes 4194320 | tf_op jit(solution)/shard_map/all_gather | solution.py:87
  95.1 2.2 copy-done.1
  97.3 1.3 shard_map.68
  98.6 23.0 %all_to_all.41 = bf16[32,128,128]{2,1,0:T(8,128)(2,1)S(1)} all-to-all(bf16[32,128,128]{2,1,0:T(8,128)(2,1)S(1)} %shard_map.68), channel_id=1, replica_groups=mesh['x'=4,'c'=2,'z'=8,'y'=4] {'x','c','y'}, dimensions={0} | all-to-all | bytes 2097152 | tf_op jit(solution)/shard_map/all_to_all | solution.py:61
  121.6 0.2 reduce_sum.24
  121.7 1.2 broadcast_in_dim.4
  122.9 5.2 %all-to-all-start.2 = ((bf16[32,128,128]{2,1,0:T(8,128)(2,1)}), bf16[32,128,128]{2,1,0:T(8,128)(2,1)S(1)}, u32[]{:S(2)}, u32[]{:S(2)}) async-start(bf16[32,128,128]{2,1,0:T(8,128)(2,1)} %broadcast_in_dim.4), calls=%async_computation.2 | async-start | bytes 2097152 | tf_op jit(solution)/shard_map/all_to_all | solution.py:63
  128.2 0.0 reduce-scatter.5.cloned.1.call-start
  128.2 0.1 copy.30.weight_ref
  128.4 22.6 %all-gather.5.cloned.1.call-done = bf16[8192,256]{1,0:T(8,128)(2,1)} async-done(((bf16[1024,256]{1,0:T(8,128)(2,1)}), bf16[8192,256]{1,0:T(8,128)(2,1)}) %all-gather.5.cloned.1.call-update) | async-done | bytes 4194320 | tf_op jit(solution)/shard_map/all_gather | solution.py:87
  150.9 7.6 %shard_map.69 = (bf16[32,128,128]{2,1,0:T(8,128)(2,1)S(1)}, bf16[64,128,256]{2,1,0:T(8,128)(2,1)}) custom-call(s32[4,8]{1,0:T(4,128)S(1)} %reshape.60.ids_ref, bf16[512,256]{1,0:T(8,128)(2,1)S(1)} %collective-permute-done.tok_ref, f32[512,1]{1,0:T(8,128)S(1)} %copy.30.weight_ref, bf16[32,128,128]{2,1,0:T(8,128)(2,1)S(1)} %all-to-all-done.2.codes_ref, ...), custom_call_target="tpu_custom_call" | custom-call | tf_op jit(solution)/shard_map/pallas_call | solution.py:113
  158.5 0.0 reduce-scatter.5.cloned.1.call-update
  158.6 0.0 reduce-scatter.3.cloned.1.call-start
  158.6 23.0 %all_to_all.42 = bf16[32,128,128]{2,1,0:T(8,128)(2,1)S(1)} all-to-all(bf16[32,128,128]{2,1,0:T(8,128)(2,1)S(1)} %get-tuple-element.10), channel_id=1, replica_groups=mesh['x'=4,'c'=2,'z'=8,'y'=4] {'x','c','y'}, dimensions={0} | all-to-all | bytes 2097152 | tf_op jit(solution)/shard_map/all_to_all | solution.py:61
  181.6 0.2 reduce_sum.25
  181.8 0.2 broadcast_in_dim.5
  182.0 20.7 %all_to_all.43.codes_ref = bf16[32,128,128]{2,1,0:T(8,128)(2,1)S(1)} all-to-all(bf16[32,128,128]{2,1,0:T(8,128)(2,1)S(1)} %broadcast_in_dim.5), channel_id=1, replica_groups=mesh['x'=4,'c'=2,'z'=8,'y'=4] {'x','c','y'}, dimensions={0} | all-to-all | bytes 2097152 | tf_op jit(solution)/shard_map/all_to_all | solution.py:63
  202.7 2.4 shard_map.70
  205.1 2.0 copy-done
  207.0 0.0 reduce-scatter.3.cloned.1.call-update
  207.1 5.6 %reduce-scatter.5.cloned.1.call-done = bf16[1024,256]{1,0:T(8,128)(2,1)} async-done(((bf16[8192,256]{1,0:T(8,128)(2,1)}), bf16[1024,256]{1,0:T(8,128)(2,1)}) %reduce-scatter.5.cloned.1.call-update) | async-done | bytes 524304 | tf_op jit(solution)/shard_map/reduce_scatter | solution.py:91
  212.6 13.8 %all_to_all.44 = bf16[4,256,256]{2,1,0:T(8,128)(2,1)S(1)} all-to-all(bf16[4,256,256]{2,1,0:T(8,128)(2,1)} %bitcast.30), channel_id=1, replica_groups=mesh['x'=4,'c'=2,'z'=8,'y'=4] {'y'}, dimensions={0} | all-to-all | bytes 1048576 | tf_op jit(solution)/shard_map/all_to_all | solution.py:92
  226.4 42.6 %reduce-scatter.3.cloned.1.call-done = bf16[1024,256]{1,0:T(8,128)(2,1)} async-done(((bf16[8192,256]{1,0:T(8,128)(2,1)}), bf16[1024,256]{1,0:T(8,128)(2,1)}) %reduce-scatter.3.cloned.1.call-update) | async-done | bytes 524304 | tf_op jit(solution)/shard_map/reduce_scatter | solution.py:91
  269.0 4.3 %all-to-all-start.6 = ((bf16[4,256,256]{2,1,0:T(8,128)(2,1)}), bf16[4,256,256]{2,1,0:T(8,128)(2,1)S(1)}, u32[]{:S(2)}, u32[]{:S(2)}) async-start(bf16[4,256,256]{2,1,0:T(8,128)(2,1)} %bitcast.31), calls=%async_computation.7 | async-start | bytes 1048576 | tf_op jit(solution)/shard_map/all_to_all | solution.py:92
  273.3 0.2 copy.32
  273.5 0.1 convert_element_type.35
  273.6 1.3 copy.34
  274.9 7.9 %all-to-all-done.6 = bf16[4,256,256]{2,1,0:T(8,128)(2,1)S(1)} async-done(((bf16[4,256,256]{2,1,0:T(8,128)(2,1)}), bf16[4,256,256]{2,1,0:T(8,128)(2,1)S(1)}, u32[]{:S(2)}, u32[]{:S(2)}) %all-to-all-start.6) | async-done | bytes 524320 | tf_op jit(solution)/shard_map/all_to_all | solution.py:92
  282.8 0.2 copy.31
  283.0 0.1 convert_element_type.34
  283.1 1.3 copy.33
  (13 shorter events, 0.0 us)
Async XLA Ops:
  7.2 6.8 %copy-start.4 = (bf16[512,256]{1,0:T(8,128)(2,1)S(1)}, bf16[512,256]{1,0:T(8,128)(2,1)}, u32[]{:S(2)}) copy-start(bf16[512,256]{1,0:T(8,128)(2,1)} %param.5) | copy-start | bytes 786436
  7.2 12.0 %copy-start.2 = (s32[4,8]{1,0:T(4,128)S(1)}, s32[4,8]{1,0:T(4,128)}, u32[]{:S(2)}) copy-start(s32[4,8]{1,0:T(4,128)} %param.8) | copy-start | bytes 388
  7.2 12.1 %copy-start.3 = (s32[512]{0:T(512)S(1)}, s32[512]{0:T(512)}, u32[]{:S(2)}) copy-start(s32[512]{0:T(512)} %param.9) | copy-start | bytes 6148
  9.5 13.9 %all-to-all-start = ((bf16[4,256,256]{1,2,0:T(8,128)(2,1)}), bf16[4,256,256]{1,2,0:T(8,128)(2,1)S(1)}, u32[]{:S(2)}, u32[]{:S(2)}) async-start(bf16[4,256,256]{1,2,0:T(8,128)(2,1)} %bitcast.1), calls=%async_computation | async-start | bytes 1048576 | tf_op jit(solution)/shard_map/all_to_all | solution.py:84
  14.0 81.1 %all-gather.3.cloned.1.call-start = ((), (), s32[]{:S(2)}) async-start(), calls=%async_computation.10 | async-start | bytes 4718592 | tf_op jit(solution)/shard_map/all_gather | solution.py:87
  14.0 24.2 %collective-permute-start = (bf16[512,256]{1,0:T(8,128)(2,1)S(1)}, bf16[512,256]{1,0:T(8,128)(2,1)S(1)}, u32[]{:S(2)}, u32[]{:S(2)}) collective-permute-start(bf16[512,256]{1,0:T(8,128)(2,1)S(1)} %copy-done.4), channel_id=1, source_target_pairs={{0,0},{4,32},{8,64},{12,96},{16,128},{20,160},{24,192},{28,224},{3... | collective-permute-start | bytes 786440 | tf_op jit(solution)/shard_map/ppermute | solution.py:77
  19.2 19.0 %collective-permute-start.1 = (s32[544]{0:T(1024)S(1)}, s32[544]{0:T(1024)S(1)}, u32[]{:S(2)}, u32[]{:S(2)}) collective-permute-start(s32[544]{0:T(1024)S(1)} %pad_add_fusion), channel_id=1, source_target_pairs={{0,0},{4,32},{8,64},{12,96},{16,128},{20,160},{24,192},{28,224},{3... | collective-permute-start | bytes 6536 | tf_op jit(solution)/shard_map/ppermute | solution.py:79
  38.3 112.7 %all-gather.5.cloned.1.call-start = ((), (), s32[]{:S(2)}) async-start(), calls=%async_computation.11 | async-start | bytes 4718592 | tf_op jit(solution)/shard_map/all_gather | solution.py:87
  95.1 2.2 copy-start.1
  122.9 28.0 %all-to-all-start.2 = ((bf16[32,128,128]{2,1,0:T(8,128)(2,1)}), bf16[32,128,128]{2,1,0:T(8,128)(2,1)S(1)}, u32[]{:S(2)}, u32[]{:S(2)}) async-start(bf16[32,128,128]{2,1,0:T(8,128)(2,1)} %broadcast_in_dim.4), calls=%async_computation.2 | async-start | bytes 2097152 | tf_op jit(solution)/shard_map/all_to_all | solution.py:63
  128.2 84.5 %reduce-scatter.5.cloned.1.call-start = ((), (), s32[]{:S(2)}) async-start(), calls=%async_computation.13 | async-start | bytes 4718592 | tf_op jit(solution)/shard_map/reduce_scatter | solution.py:91
  158.6 110.4 %reduce-scatter.3.cloned.1.call-start = ((), (), s32[]{:S(2)}) async-start(), calls=%async_computation.12 | async-start | bytes 4718592 | tf_op jit(solution)/shard_map/reduce_scatter | solution.py:91
  205.1 2.0 copy-start
  269.0 13.8 %all-to-all-start.6 = ((bf16[4,256,256]{2,1,0:T(8,128)(2,1)}), bf16[4,256,256]{2,1,0:T(8,128)(2,1)S(1)}, u32[]{:S(2)}, u32[]{:S(2)}) async-start(bf16[4,256,256]{2,1,0:T(8,128)(2,1)} %bitcast.31), calls=%async_computation.7 | async-start | bytes 1048576 | tf_op jit(solution)/shard_map/all_to_all | solution.py:92
Sparse Core Ops, SparseCore 0:
  38.4 56.6 all-gather.2
  97.5 53.4 all-gather.4
  158.7 53.8 reduce-scatter.4
  215.0 53.9 reduce-scatter.2

commit v3 on v2

--- a/solution.py
+++ b/solution.py
@@ -74,14 +74,17 @@
     d = lax.axis_index(("x", "c"))
 
     swap = [(g * nz + z, z * nz + g) for g in range(nd) for z in range(nz)]
-    tok = lax.ppermute(tokens, ("x", "c", "z"), swap)
     small = jnp.concatenate([counts, active_blocks.reshape(-1)])
     small = lax.ppermute(small, ("x", "c", "z"), swap)
+    weights = small[:tok_dev].astype(jnp.float32)[:, None] / BLOCK
+    ids = small[tok_dev:].reshape(tb, act)
 
     def own_features(weight):
-        mine = lax.dynamic_slice_in_dim(weight, d * (ny * width), ny * width, axis=1)
-        mine = mine.reshape(rows, ny, width).transpose(1, 0, 2)
-        return lax.all_to_all(mine, "y", 0, 0, tiled=True).reshape(ny * rows, width)
+        quarter = [
+            lax.dynamic_slice_in_dim(weight, (d * ny + j) * width, width, axis=1) for j in range(ny)
+        ]
+        got = lax.all_to_all(jnp.stack(quarter), "y", 0, 0, tiled=True)
+        return got.reshape(ny * rows, width)
 
     def all_rows(mine):
         whole = lax.all_gather(mine, "z", axis=0, tiled=True)
@@ -90,13 +93,16 @@
     def own_rows(grad):
         part = lax.psum_scatter(grad.reshape(nz * ny * rows, width), "z", scatter_dimension=0, tiled=True)
         part = lax.all_to_all(part.reshape(ny, rows, width), "y", 0, 0, tiled=True)
-        return part.transpose(1, 0, 2).reshape(rows, ny * width).astype(jnp.float32)
+        return jnp.concatenate([part[j] for j in range(ny)], axis=1).astype(jnp.float32)
 
-    mine, tok, small = lax.optimization_barrier((own_features(enc_weight), tok, small))
+    mine = own_features(enc_weight)
     enc = all_rows(mine)
+    tokens, dec_weight, mine = lax.optimization_barrier((tokens, dec_weight, mine))
     dec = all_rows(own_features(dec_weight))
-    weights = small[:tok_dev].astype(jnp.float32)[:, None] / BLOCK
-    ids = small[tok_dev:].reshape(tb, act)
+    tok = tokens.reshape(nd, tok_dev // nd, width)
+    for axes in (("x", "c"), "z", ("x", "c")):
+        tok = lax.all_to_all(tok, axes, 0, 0, tiled=True)
+    tok = tok.reshape(tok_dev, width)
 
     pairs = jax.ShapeDtypeStruct((tb * act, BLOCK, BLOCK), jnp.bfloat16)
     grads = jax.ShapeDtypeStruct((lat_blocks, BLOCK, width), jnp.bfloat16)

time: 292 us -> 280 us (0.959)
  waiting for transfers between devices: 137 us -> 85.7 us
  blocking collectives: 92.9 us -> 141 us
  starting transfers between devices: 21.7 us -> 16.1 us
  local copies, waits for them, and re-layouts: 13.4 us -> 8.27 us
    all_to_all x1 -> x4, blocking collectives: 12.5 us -> 59.8 us  [the longest x2 34.3 us: per_device(): tok = lax.all_to_all(tok, axes, 0, 0, tiled=True)]
    all_gather x2, waiting for transfers between devices: 65.6 us -> 23.7 us  [all_rows(): whole = lax.all_gather(mine, 'z', axis=0, tiled=True)]
    ppermute x1, waiting for transfers between devices: 13.8 us -> 5.43 us  [per_device(): small = lax.ppermute(small, ('x', 'c', 'z'), swap)]
    ppermute x1 -> x0, starting transfers between devices: 5.15 us -> none  [per_device(): tok = lax.ppermute(tokens, ('x', 'c', 'z'), swap)]
    unnamed x14 -> x10, local copies, waits for them, and re-layouts: 7.98 us -> 4.16 us
  transfers between devices with their start and end apart: 9 -> 8, of which waited for: 7 -> 6; matrix products, arithmetic and copies ran while one was open for 2% -> 2% of each run, Pallas kernels for 1% -> 1%
where the time goes in v3:
time: 280 us; the launch traced here: 279 us
  blocking collectives  141 us (50%)
  waiting for transfers between devices  85.7 us (31%)
  starting transfers between devices  16.1 us (6%)
  between operations  13.9 us (5%)
  Pallas kernels  11.3 us (4%)
  local copies, waits for them, and re-layouts  8.27 us (3%)
    reduce_scatter x2, waiting for transfers between devices, own_rows(): lax.psum_scatter(grad.reshape(nz * ny * rows, width), 'z', scatter_dimens...  48.1 us
    all_to_all x2, blocking collectives, all_sum(): got = lax.all_to_all(part, axes, 0, 0, tiled=True)  46.5 us
    all_to_all x2, blocking collectives, per_device(): tok = lax.all_to_all(tok, axes, 0, 0, tiled=True)  34.3 us
    all_to_all x2, blocking collectives, own_features(): got = lax.all_to_all(jnp.stack(quarter), 'y', 0, 0, tiled=True)  25.5 us
    all_gather x2, waiting for transfers between devices, all_rows(): whole = lax.all_gather(mine, 'z', axis=0, tiled=True)  23.7 us
    all_to_all x1, blocking collectives, all_sum(): lax.all_to_all(jnp.broadcast_to(mine[None], part.shape), axes, 0, 0, tile...  20.7 us
    all_to_all x1, blocking collectives, own_rows(): part = lax.all_to_all(part.reshape(ny, rows, width), 'y', 0, 0, tiled=True)  13.8 us
    all_to_all x1, waiting for transfers between devices, own_rows(): part = lax.all_to_all(part.reshape(ny, rows, width), 'y', 0, 0, tiled=True)  8.4 us
  transfers between devices with their start and end apart: 8, of which 6 were waited for; matrix products, arithmetic and copies ran while one was open for 2% of the time, Pallas kernels for 1%

profile of v3, /device:TPU:2, one launch (start us, length us, event | category | flops | bytes accessed | tf_op | source)
XLA Modules:
  0.0 278.8 jit_solution(3825998288109446194)
XLA Ops:
  7.2 0.0 all-gather.3.cloned.1.call-start
  7.2 1.1 dynamic-slice_bitcast_fusion.7
  8.4 0.0 copy-start.3
  8.4 0.0 copy-start.4
  8.4 0.1 pad_maximum_fusion
  8.5 13.8 %all_to_all.55 = bf16[4,256,256]{2,1,0:T(8,128)(2,1)} all-to-all(bf16[4,256,256]{2,1,0:T(8,128)(2,1)S(1)} %pad_maximum_fusion), channel_id=1, replica_groups=mesh['x'=4,'c'=2,'z'=8,'y'=4] {'y'}, dimensions={0} | all-to-all | bytes 1048576 | tf_op jit(solution)/shard_map/all_to_all | solution.py:86
  22.3 0.0 all-gather.3.cloned.1.call-update
  22.4 0.0 all-gather.5.cloned.1.call-start
  22.4 1.1 dynamic-slice_bitcast_fusion.3
  23.6 0.1 pad_maximum_fusion.1
  23.6 11.7 %all_to_all.56 = bf16[4,256,256]{2,1,0:T(8,128)(2,1)} all-to-all(bf16[4,256,256]{2,1,0:T(8,128)(2,1)S(1)} %pad_maximum_fusion.1), channel_id=1, replica_groups=mesh['x'=4,'c'=2,'z'=8,'y'=4] {'y'}, dimensions={0} | all-to-all | bytes 1048576 | tf_op jit(solution)/shard_map/all_to_all | solution.py:86
  35.3 0.0 all-gather.5.cloned.1.call-update
  35.3 10.7 %all_to_all.57 = bf16[8,64,256]{2,1,0:T(8,128)(2,1)S(1)} all-to-all(bf16[8,64,256]{2,1,0:T(8,128)(2,1)S(1)} %bitcast.54), channel_id=1, replica_groups=mesh['x'=4,'c'=2,'z'=8,'y'=4] {'x','c'}, dimensions={0} | all-to-all | bytes 524288 | tf_op jit(solution)/shard_map/all_to_all | solution.py:104
  46.0 23.6 %all_to_all.58 = bf16[8,64,256]{2,1,0:T(8,128)(2,1)} all-to-all(bf16[8,64,256]{2,1,0:T(8,128)(2,1)S(1)} %all_to_all.57), channel_id=1, replica_groups=mesh['x'=4,'c'=2,'z'=8,'y'=4] {'z'}, dimensions={0} | all-to-all | bytes 524288 | tf_op jit(solution)/shard_map/all_to_all | solution.py:104
  69.6 4.6 %all-to-all-start.3 = ((bf16[8,64,256]{2,1,0:T(8,128)(2,1)}), bf16[8,64,256]{2,1,0:T(8,128)(2,1)S(1)}, u32[]{:S(2)}, u32[]{:S(2)}) async-start(bf16[8,64,256]{2,1,0:T(8,128)(2,1)} %all_to_all.58), calls=%async_computation.3 | async-start | bytes 524288 | tf_op jit(solution)/shard_map/all_to_all | solution.py:104
  74.2 0.1 reshape.51
  74.3 1.9 collective-permute-start
  76.2 5.4 %collective-permute-done = s32[544]{0:T(1024)S(1)} collective-permute-done((s32[544]{0:T(1024)S(1)}, s32[544]{0:T(1024)S(1)}, u32[]{:S(2)}, u32[]{:S(2)}) %collective-permute-start) | collective-permute-done | bytes 2208 | tf_op jit(solution)/shard_map/ppermute | solution.py:78
  81.7 0.1 reshape.52.ids_ref
  81.8 0.0 all-to-all-done.3
  81.8 2.2 all-gather.3.cloned.1.call-done
  83.9 2.2 copy-done.1
  86.1 1.3 shard_map.68
  87.4 23.5 %all_to_all.59 = bf16[32,128,128]{2,1,0:T(8,128)(2,1)S(1)} all-to-all(bf16[32,128,128]{2,1,0:T(8,128)(2,1)S(1)} %shard_map.68), channel_id=1, replica_groups=mesh['x'=4,'c'=2,'z'=8,'y'=4] {'x','c','y'}, dimensions={0} | all-to-all | bytes 2097152 | tf_op jit(solution)/shard_map/all_to_all | solution.py:61
  110.9 0.2 reduce_sum.24
  111.1 1.2 broadcast_in_dim.4
  112.3 5.2 %all-to-all-start.5 = ((bf16[32,128,128]{2,1,0:T(8,128)(2,1)}), bf16[32,128,128]{2,1,0:T(8,128)(2,1)S(1)}, u32[]{:S(2)}, u32[]{:S(2)}) async-start(bf16[32,128,128]{2,1,0:T(8,128)(2,1)} %broadcast_in_dim.4), calls=%async_computation.5 | async-start | bytes 2097152 | tf_op jit(solution)/shard_map/all_to_all | solution.py:63
  117.5 0.0 reduce-scatter.5.cloned.1.call-start
  117.6 0.1 copy.7.weight_ref
  117.7 21.5 %all-gather.5.cloned.1.call-done = bf16[8192,256]{1,0:T(8,128)(2,1)} async-done(((bf16[1024,256]{1,0:T(8,128)(2,1)}), bf16[8192,256]{1,0:T(8,128)(2,1)}) %all-gather.5.cloned.1.call-update) | async-done | bytes 4194320 | tf_op jit(solution)/shard_map/all_gather | solution.py:90
  139.2 0.0 all-to-all-done.5.codes_ref
  139.2 7.6 %shard_map.69 = (bf16[32,128,128]{2,1,0:T(8,128)(2,1)S(1)}, bf16[64,128,256]{2,1,0:T(8,128)(2,1)}) custom-call(s32[4,8]{1,0:T(4,128)S(1)} %reshape.52.ids_ref, bf16[512,256]{1,0:T(8,128)(2,1)S(1)} %bitcast.46, f32[512,1]{1,0:T(8,128)S(1)} %copy.7.weight_ref, bf16[32,128,128]{2,1,0:T(8,128)(2,1)S(1)} %all-to-all-done.5.codes_ref, bf16[64,128,256]{2,1,0:T(8,128)(2,1)} %bitcast.48), custom_call_target="tpu_custom_call" | custom-call | tf_op jit(solution)/shard_map/pallas_call | solution.py:119
  146.9 0.0 reduce-scatter.5.cloned.1.call-update
  146.9 0.0 reduce-scatter.3.cloned.1.call-start
  146.9 23.0 %all_to_all.60 = bf16[32,128,128]{2,1,0:T(8,128)(2,1)S(1)} all-to-all(bf16[32,128,128]{2,1,0:T(8,128)(2,1)S(1)} %get-tuple-element.8), channel_id=1, replica_groups=mesh['x'=4,'c'=2,'z'=8,'y'=4] {'x','c','y'}, dimensions={0} | all-to-all | bytes 2097152 | tf_op jit(solution)/shard_map/all_to_all | solution.py:61
  169.9 0.2 reduce_sum.25
  170.1 0.2 broadcast_in_dim.5
  170.3 20.7 %all_to_all.61.codes_ref = bf16[32,128,128]{2,1,0:T(8,128)(2,1)S(1)} all-to-all(bf16[32,128,128]{2,1,0:T(8,128)(2,1)S(1)} %broadcast_in_dim.5), channel_id=1, replica_groups=mesh['x'=4,'c'=2,'z'=8,'y'=4] {'x','c','y'}, dimensions={0} | all-to-all | bytes 2097152 | tf_op jit(solution)/shard_map/all_to_all | solution.py:63
  191.0 2.4 shard_map.70
  193.4 2.0 copy-done
  195.4 0.0 reduce-scatter.3.cloned.1.call-update
  195.4 5.6 %reduce-scatter.5.cloned.1.call-done = bf16[1024,256]{1,0:T(8,128)(2,1)} async-done(((bf16[8192,256]{1,0:T(8,128)(2,1)}), bf16[1024,256]{1,0:T(8,128)(2,1)}) %reduce-scatter.5.cloned.1.call-update) | async-done | bytes 524304 | tf_op jit(solution)/shard_map/reduce_scatter | solution.py:94
  201.0 13.8 %all_to_all.62 = bf16[4,256,256]{2,1,0:T(8,128)(2,1)S(1)} all-to-all(bf16[4,256,256]{2,1,0:T(8,128)(2,1)} %bitcast.52), channel_id=1, replica_groups=mesh['x'=4,'c'=2,'z'=8,'y'=4] {'y'}, dimensions={0} | all-to-all | bytes 1048576 | tf_op jit(solution)/shard_map/all_to_all | solution.py:95
  214.8 42.6 %reduce-scatter.3.cloned.1.call-done = bf16[1024,256]{1,0:T(8,128)(2,1)} async-done(((bf16[8192,256]{1,0:T(8,128)(2,1)}), bf16[1024,256]{1,0:T(8,128)(2,1)}) %reduce-scatter.3.cloned.1.call-update) | async-done | bytes 524304 | tf_op jit(solution)/shard_map/reduce_scatter | solution.py:94
  257.3 4.3 %all-to-all-start.9 = ((bf16[4,256,256]{2,1,0:T(8,128)(2,1)}), bf16[4,256,256]{2,1,0:T(8,128)(2,1)S(1)}, u32[]{:S(2)}, u32[]{:S(2)}) async-start(bf16[4,256,256]{2,1,0:T(8,128)(2,1)} %bitcast.53), calls=%async_computation.10 | async-start | bytes 1048576 | tf_op jit(solution)/shard_map/all_to_all | solution.py:95
  261.6 1.1 maximum_convert_fusion.1
  262.7 8.4 %all-to-all-done.9 = bf16[4,256,256]{2,1,0:T(8,128)(2,1)S(1)} async-done(((bf16[4,256,256]{2,1,0:T(8,128)(2,1)}), bf16[4,256,256]{2,1,0:T(8,128)(2,1)S(1)}, u32[]{:S(2)}, u32[]{:S(2)}) %all-to-all-start.9) | async-done | bytes 524320 | tf_op jit(solution)/shard_map/all_to_all | solution.py:95
  271.2 1.1 maximum_convert_fusion
  (11 shorter events, 0.1 us)
Async XLA Ops:
  7.2 28.2 %copy-start.2 = (bf16[512,256]{1,0:T(8,128)(2,1)S(1)}, bf16[512,256]{1,0:T(8,128)(2,1)}, u32[]{:S(2)}) copy-start(bf16[512,256]{1,0:T(8,128)(2,1)} %param.5) | copy-start | bytes 786436
  7.2 76.7 %all-gather.3.cloned.1.call-start = ((), (), s32[]{:S(2)}) async-start(), calls=%async_computation.13 | async-start | bytes 4718592 | tf_op jit(solution)/shard_map/all_gather | solution.py:90
  8.4 65.8 %copy-start.3 = (s32[4,8]{1,0:T(4,128)S(1)}, s32[4,8]{1,0:T(4,128)}, u32[]{:S(2)}) copy-start(s32[4,8]{1,0:T(4,128)} %param.8) | copy-start | bytes 388
  8.4 65.9 %copy-start.4 = (s32[512]{0:T(512)S(1)}, s32[512]{0:T(512)}, u32[]{:S(2)}) copy-start(s32[512]{0:T(512)} %param.9) | copy-start | bytes 6148
  22.4 116.9 %all-gather.5.cloned.1.call-start = ((), (), s32[]{:S(2)}) async-start(), calls=%async_computation.14 | async-start | bytes 4718592 | tf_op jit(solution)/shard_map/all_gather | solution.py:90
  69.6 12.1 %all-to-all-start.3 = ((bf16[8,64,256]{2,1,0:T(8,128)(2,1)}), bf16[8,64,256]{2,1,0:T(8,128)(2,1)S(1)}, u32[]{:S(2)}, u32[]{:S(2)}) async-start(bf16[8,64,256]{2,1,0:T(8,128)(2,1)} %all_to_all.58), calls=%async_computation.3 | async-start | bytes 524288 | tf_op jit(solution)/shard_map/all_to_all | solution.py:104
  74.3 7.4 %collective-permute-start = (s32[544]{0:T(1024)S(1)}, s32[544]{0:T(1024)S(1)}, u32[]{:S(2)}, u32[]{:S(2)}) collective-permute-start(s32[544]{0:T(1024)S(1)} %pad_add_fusion), channel_id=1, source_target_pairs={{0,0},{4,32},{8,64},{12,96},{16,128},{20,160},{24,192},{28,224},{3... | collective-permute-start | bytes 6536 | tf_op jit(solution)/shard_map/ppermute | solution.py:78
  83.9 2.2 copy-start.1
  112.3 26.9 %all-to-all-start.5 = ((bf16[32,128,128]{2,1,0:T(8,128)(2,1)}), bf16[32,128,128]{2,1,0:T(8,128)(2,1)S(1)}, u32[]{:S(2)}, u32[]{:S(2)}) async-start(bf16[32,128,128]{2,1,0:T(8,128)(2,1)} %broadcast_in_dim.4), calls=%async_computation.5 | async-start | bytes 2097152 | tf_op jit(solution)/shard_map/all_to_all | solution.py:63
  117.5 83.4 %reduce-scatter.5.cloned.1.call-start = ((), (), s32[]{:S(2)}) async-start(), calls=%async_computation.16 | async-start | bytes 4718592 | tf_op jit(solution)/shard_map/reduce_scatter | solution.py:94
  146.9 110.4 %reduce-scatter.3.cloned.1.call-start = ((), (), s32[]{:S(2)}) async-start(), calls=%async_computation.15 | async-start | bytes 4718592 | tf_op jit(solution)/shard_map/reduce_scatter | solution.py:94
  193.4 2.0 copy-start
  257.3 13.8 %all-to-all-start.9 = ((bf16[4,256,256]{2,1,0:T(8,128)(2,1)}), bf16[4,256,256]{2,1,0:T(8,128)(2,1)S(1)}, u32[]{:S(2)}, u32[]{:S(2)}) async-start(bf16[4,256,256]{2,1,0:T(8,128)(2,1)} %bitcast.53), calls=%async_computation.10 | async-start | bytes 1048576 | tf_op jit(solution)/shard_map/all_to_all | solution.py:95
Sparse Core Ops, SparseCore 0:
  22.5 61.4 all-gather.2
  85.7 53.4 all-gather.4
  147.0 53.8 reduce-scatter.4
  203.4 53.9 reduce-scatter.2

commit v4 on v0

v4 whole, which is shorter than its diff:
```python
import functools

import jax
import jax.numpy as jnp
import numpy as np
from jax import lax
from jax.experimental import pallas as pl
from jax.experimental.pallas import tpu as pltpu
from jax.sharding import Mesh
from jax.sharding import PartitionSpec as P

BLOCK = 128
VMEM = pltpu.CompilerParams(vmem_limit_bytes=48 * 1024 * 1024)
ALL_VMEM = pltpu.CompilerParams(vmem_limit_bytes=61 * 1024 * 1024)
NT = (((1,), (1,)), ((), ()))
TN = (((0,), (0,)), ((), ()))
SMEM_SPEC = pl.BlockSpec(memory_space=pltpu.SMEM)
VMEM_SPEC = pl.BlockSpec(memory_space=pltpu.VMEM)


def dot(left, right, dims):
    return lax.dot_general(left, right, dims, preferred_element_type=jnp.float32)


def split_kernel(ny, sub, d_ref, *refs):
    out_ref = refs[-1]
    for z, in_ref in enumerate(refs[:-1]):
        for y in range(ny):
            for i in range(in_ref.shape[0] // BLOCK):
                at = i * BLOCK + y * sub
                out_ref[z * ny + y, i] = in_ref[at : at + sub, :]


def select(ids_ref, weight_ref, t, act, sel_ref):
    pieces, _, sub, lanes = weight_ref.shape
    for a in range(act):
        for p in range(pieces):
            sel_ref[t, a * sub : (a + 1) * sub, p * lanes : (p + 1) * lanes] = weight_ref[p, ids_ref[t, a]]


def token_rows(tok_ref, at):
    return jnp.concatenate([tok_ref[q, at, :] for q in range(tok_ref.shape[0])], axis=1)


def block(t):
    return slice(t * BLOCK, (t + 1) * BLOCK)


def pre_kernel(tb, act, ids_ref, tok_ref, enc_ref, out_ref, sel_ref):
    for t in range(tb):
        select(ids_ref, enc_ref, t, act, sel_ref)
        out_ref[block(t), :] = dot(token_rows(tok_ref, block(t)), sel_ref[t], NT).astype(jnp.bfloat16)


def recon_kernel(tb, act, ids_ref, codes_ref, dec_ref, out_ref, sel_ref):
    for t in range(tb):
        select(ids_ref, dec_ref, t, act, sel_ref)
        out_ref[t] = jnp.dot(
            codes_ref[block(t), :], sel_ref[t], preferred_element_type=jnp.float32
        ).astype(jnp.bfloat16)


def error_kernel(y_ref, tok_ref, weight_ref, recon_ref, out_ref):
    at = pl.ds(pl.multiple_of(y_ref[0] * BLOCK, BLOCK), BLOCK)
    recon = recon_ref[0].astype(jnp.float32)
    for k in range(1, recon_ref.shape[0]):
        recon += recon_ref[k].astype(jnp.float32)
    gout = weight_ref[at, :] * (recon - token_rows(tok_ref, at).astype(jnp.float32))
    gout = gout.astype(jnp.bfloat16)
    for k in range(out_ref.shape[0]):
        out_ref[k] = gout


def sum_rows(tb, act, ids_ref, codes_ref, rows_of, prod_ref, acc_ref, out_ref):
    pieces, blocks, sub, lanes = acc_ref.shape
    acc_ref[...] = jnp.zeros_like(acc_ref)
    for t in range(tb):
        prod_ref[...] = dot(codes_ref[block(t), :], rows_of(t), TN)
        for a in range(act):
            for p in range(pieces):
                acc_ref[p, ids_ref[t, a]] += prod_ref[a * sub : (a + 1) * sub, p * lanes : (p + 1) * lanes]

    @pl.loop(0, blocks)
    def _(b):
        for p in range(pieces):
            out_ref[p, b] = acc_ref[p, b].astype(jnp.bfloat16)


def dec_kernel(tb, act, ids_ref, codes_ref, gout_ref, sel_ref, part_ref, grad_ref, prod_ref, acc_ref):
    for t in range(tb):
        part_ref[block(t), :] = dot(gout_ref[t], sel_ref[t], NT).astype(jnp.bfloat16)
    sum_rows(tb, act, ids_ref, codes_ref, lambda t: gout_ref[t], prod_ref, acc_ref, grad_ref)


def enc_kernel(tb, act, ids_ref, codes_ref, tok_ref, grad_ref, prod_ref, acc_ref):
    sum_rows(tb, act, ids_ref, codes_ref, lambda t: token_rows(tok_ref, block(t)), prod_ref, acc_ref, grad_ref)


def join_kernel(in_ref, out_ref):
    pieces, ny, blocks, sub, lanes = in_ref.shape
    for p in range(pieces):
        for y in range(ny):
            for i in range(blocks):
                at = i * BLOCK + y * sub
                out_ref[at : at + sub, p * lanes : (p + 1) * lanes] = in_ref[p, y, i].astype(jnp.float32)


def call(kernel, out_shape, n_smem, n_vmem, scratch=()):
    many = isinstance(out_shape, tuple)
    return pl.pallas_call(
        kernel,
        out_shape=out_shape,
        in_specs=[SMEM_SPEC] * n_smem + [VMEM_SPEC] * n_vmem,
        out_specs=(VMEM_SPEC,) * len(out_shape) if many else VMEM_SPEC,
        scratch_shapes=list(scratch),
        compiler_params=VMEM,
    )


def all_sum(part, axis, n):
    got = lax.all_to_all(part.reshape(n, -1, part.shape[1]), axis, 0, 0, tiled=True)
    mine = jnp.sum(got.astype(jnp.float32), axis=0).astype(part.dtype)
    got = lax.all_to_all(jnp.broadcast_to(mine[None], got.shape), axis, 0, 0, tiled=True)
    return got.reshape(part.shape)


def per_device(tokens, enc_weight, dec_weight, active_blocks, counts, *, sizes):
    nd, nz, ny = sizes["x"] * sizes["c"], sizes["z"], sizes["y"]
    dp, latent = ("x", "c"), ("z", "y")
    tok_dev, width = tokens.shape
    tb, act = active_blocks.shape
    rows, model = enc_weight.shape
    feats = model // nz
    lanes = feats // nd
    sub = BLOCK // ny
    mine_blocks = rows // BLOCK
    blocks = nz * ny * mine_blocks
    d = lax.axis_index(dp).astype(jnp.int32).reshape(1)
    y = lax.axis_index("y").astype(jnp.int32).reshape(1)
    weights = counts.astype(jnp.float32)[:, None] / BLOCK

    def spread(weight):
        out = (nz * ny, mine_blocks, sub, lanes)
        pieces = pl.pallas_call(
            functools.partial(split_kernel, ny, sub),
            out_shape=jax.ShapeDtypeStruct(out, jnp.bfloat16),
            grid_spec=pltpu.PrefetchScalarGridSpec(
                num_scalar_prefetch=1,
                grid=(1,),
                in_specs=[
                    pl.BlockSpec((rows, lanes), lambda i, d_ref, z=z: (0, z * nd + d_ref[0]))
                    for z in range(nz)
                ],
                out_specs=pl.BlockSpec(out, lambda i, d_ref: (0, 0, 0, 0)),
            ),
            compiler_params=ALL_VMEM,
        )(d, *[weight] * nz)
        return lax.all_to_all(pieces, latent, 0, 0, tiled=True)

    def gather(pieces):
        whole = lax.all_gather(pieces.reshape(blocks * sub, lanes), dp, axis=0, tiled=True)
        return whole.reshape(nd, blocks, sub, lanes)

    def own(grad):
        part = lax.psum_scatter(grad.reshape(nd * blocks * sub, lanes), dp, scatter_dimension=0, tiled=True)
        part = lax.all_to_all(part.reshape(nz * ny, mine_blocks, sub, lanes), latent, 0, 0, tiled=True)
        part = lax.all_to_all(part.reshape(nz, ny, mine_blocks, sub, lanes), dp, 0, 0, tiled=True)
        return call(join_kernel, jax.ShapeDtypeStruct((rows, nd * lanes), jnp.float32), 0, 1)(part)

    mine = spread(enc_weight)
    enc = gather(mine)
    tokens, dec_weight, mine = lax.optimization_barrier((tokens, dec_weight, mine))
    dec = gather(spread(dec_weight))
    tok = lax.all_to_all(jnp.broadcast_to(tokens[None], (ny, tok_dev, width)), "y", 0, 0, tiled=True)

    half = jnp.bfloat16
    codes_like = jax.ShapeDtypeStruct((tok_dev, act * sub), half)
    sel_like = jax.ShapeDtypeStruct((tb, act * sub, feats), half)
    rows_like = jax.ShapeDtypeStruct((tb, BLOCK, feats), half)
    grad_like = jax.ShapeDtypeStruct((nd, blocks, sub, lanes), half)
    sums = (pltpu.VMEM((act * sub, feats), jnp.float32), pltpu.VMEM((nd, blocks, sub, lanes), jnp.float32))

    part = call(
        functools.partial(pre_kernel, tb, act), codes_like, 1, 2, [pltpu.VMEM(sel_like.shape, half)]
    )(active_blocks, tok, enc)
    codes = all_sum(part, "z", nz)
    recon, sel = call(functools.partial(recon_kernel, tb, act), (rows_like, sel_like), 1, 2)(
        active_blocks, codes, dec
    )
    recon = lax.all_to_all(recon, "y", 0, 0, tiled=True)
    gout = call(error_kernel, rows_like, 1, 3)(y, tok, weights, recon)
    gout = lax.all_to_all(gout, "y", 0, 0, tiled=True)
    part, group_dec = call(functools.partial(dec_kernel, tb, act), (codes_like, grad_like), 1, 3, sums)(
        active_blocks, codes, gout, sel
    )
    grad_dec = own(group_dec)
    grad_codes = all_sum(part, "z", nz)
    group_enc = call(functools.partial(enc_kernel, tb, act), grad_like, 1, 2, sums)(
        active_blocks, grad_codes, tok
    )
    grad_enc = own(group_enc)
    return (grad_enc, grad_dec)


def solution(mesh):
    fine = Mesh(np.asarray(mesh.devices).reshape(4, 2, 8, 4), ("x", "c", "z", "y"))
    dp, latent = ("x", "c"), ("z", "y")
    return jax.shard_map(
        functools.partial(per_device, sizes=dict(fine.shape)),
        mesh=fine,
        in_specs=(P(dp, latent), P(latent, None), P(latent, None), P(dp, None), P(dp)),
        out_specs=(P(latent, dp), P(latent, dp)),
        check_vma=False,
    )
```

time: 571 us -> 289 us (0.51)
  waiting for transfers between devices: 507 us -> 33.9 us
  blocking collectives: 0 us -> 198 us
  matrix products: 38.5 us -> 0 us
  Pallas kernels: 0 us -> 20.2 us
  starting transfers between devices: 0.38 us -> 14.3 us
  other arithmetic: 6.95 us -> 0.08 us
    reduce_scatter x3 -> x2, waiting for transfers between devices: 294 us -> 14.3 us  [own(): lax.psum_scatter(grad.reshape(nd * blocks * sub, lanes), dp, scatter_dime...]
    all_gather x2, waiting for transfers between devices: 212 us -> 0.01 us  [gather(): lax.all_gather(pieces.reshape(blocks * sub, lanes), dp, axis=0, tiled=True)]
    all_to_all x0 -> x10, blocking collectives: none -> 198 us  [the longest x2 56.2 us: own(): lax.all_to_all(part.reshape(nz * ny, mine_blocks, sub, lanes), latent, 0,...]
    dot_general x4 -> x0, matrix products: 38.5 us -> none  [the longest x2 25.6 us: matmul_tn(): lax.dot_general(left, right, (((0,), (0,)), ((), ())), preferred_element_...]
    pallas_call x0 -> x9, Pallas kernels: none -> 20.2 us  [the longest x1 5.66 us: per_device(): call(functools.partial(dec_kernel, tb, act), (codes_like, grad_like), 1,...]
    all_to_all x0 -> x3, waiting for transfers between devices: none -> 19.5 us  [the longest x1 11.7 us: per_device(): recon = lax.all_to_all(recon, 'y', 0, 0, tiled=True)]
    all_to_all x0 -> x3, starting transfers between devices: none -> 14.1 us  [the longest x2 10.6 us: own(): lax.all_to_all(part.reshape(nz, ny, mine_blocks, sub, lanes), dp, 0, 0, t...]
    convert_element_type x4 -> x0, other arithmetic: 6.05 us -> none  [the longest x1 2.13 us: per_device(): lax.psum_scatter(group_enc, 'dp', scatter_dimension=1, tiled=True)]
  transfers between devices with their start and end apart: 5 -> 7, of which waited for: 5 -> 4; matrix products, arithmetic and copies ran while one was open for 2% -> 0% of each run, Pallas kernels for 0% -> 3%
where the time goes in v4:
time: 289 us; the launch traced here: 286 us
  blocking collectives  198 us (69%)
  waiting for transfers between devices  33.9 us (12%)
  Pallas kernels  20.2 us (7%)
  starting transfers between devices  14.3 us (5%)
  between operations  13.9 us (5%)
  local copies, waits for them, and re-layouts  5.74 us (2%)
    all_to_all x2, blocking collectives, own(): lax.all_to_all(part.reshape(nz * ny, mine_blocks, sub, lanes), latent, 0,...  56.2 us
    all_to_all x2, blocking collectives, spread(): return lax.all_to_all(pieces, latent, 0, 0, tiled=True)  51.2 us
    all_to_all x2, blocking collectives, all_sum(): lax.all_to_all(part.reshape(n, -1, part.shape[1]), axis, 0, 0, tiled=True)  34.9 us
    all_to_all x2, blocking collectives, all_sum(): lax.all_to_all(jnp.broadcast_to(mine[None], got.shape), axis, 0, 0, tiled...  25.8 us
    all_to_all x1, blocking collectives, per_device(): lax.all_to_all(jnp.broadcast_to(tokens[None], (ny, tok_dev, width)), 'y',...  16.3 us
    reduce_scatter x2, waiting for transfers between devices, own(): lax.psum_scatter(grad.reshape(nd * blocks * sub, lanes), dp, scatter_dime...  14.3 us
    all_to_all x1, blocking collectives, per_device(): gout = lax.all_to_all(gout, 'y', 0, 0, tiled=True)  13.4 us
    all_to_all x1, waiting for transfers between devices, per_device(): recon = lax.all_to_all(recon, 'y', 0, 0, tiled=True)  11.7 us
  transfers between devices with their start and end apart: 7, of which 4 were waited for; matrix products, arithmetic and copies ran while one was open for 0% of the time, Pallas kernels for 3%

profile of v4, /device:TPU:2, one launch (start us, length us, event | category | flops | bytes accessed | tf_op | source)
XLA Modules:
  0.0 285.9 jit_solution(12052289793922677497)
XLA Ops:
  7.2 0.0 all-gather.3.cloned.1.call-start
  7.2 1.9 shard_map.68
  9.1 29.3 %all_to_all.65 = bf16[32,2,32,128]{3,2,1,0:T(8,128)(2,1)} all-to-all(bf16[32,2,32,128]{3,2,1,0:T(8,128)(2,1)} %shard_map.68), channel_id=1, replica_groups=mesh['x'=4,'c'=2,'z'=8,'y'=4] {'z','y'}, dimensions={0} | all-to-all | bytes 1048576 | tf_op jit(solution)/shard_map/all_to_all | solution.py:158
  38.4 0.0 all-gather.3.cloned.1.call-update
  38.5 0.0 copy-start.5
  38.5 0.0 all-gather.5.cloned.1.call-start
  38.5 1.9 shard_map.70
  40.5 0.0 copy-start.4
  40.5 21.9 %all_to_all.66 = bf16[32,2,32,128]{3,2,1,0:T(8,128)(2,1)} all-to-all(bf16[32,2,32,128]{3,2,1,0:T(8,128)(2,1)} %shard_map.70), channel_id=1, replica_groups=mesh['x'=4,'c'=2,'z'=8,'y'=4] {'z','y'}, dimensions={0} | all-to-all | bytes 1048576 | tf_op jit(solution)/shard_map/all_to_all | solution.py:158
  62.3 0.0 all-gather.5.cloned.1.call-update
  62.3 0.0 copy-done.5
  62.4 0.1 broadcast_in_dim.6
  62.4 16.3 %all_to_all.67.tok_ref = bf16[4,512,256]{2,1,0:T(8,128)(2,1)S(1)} all-to-all(bf16[4,512,256]{2,1,0:T(8,128)(2,1)S(1)} %broadcast_in_dim.6), channel_id=1, replica_groups=mesh['x'=4,'c'=2,'z'=8,'y'=4] {'y'}, dimensions={0} | all-to-all | bytes 2097152 | tf_op jit(solution)/shard_map/all_to_all | solution.py:174
  78.8 0.0 copy-done.4
  78.8 2.2 copy-done.1
  81.0 1.5 shard_map.69
  82.4 0.0 copy-start.6
  82.4 13.9 %all_to_all.68 = bf16[8,64,256]{2,1,0:T(8,128)(2,1)S(1)} all-to-all(bf16[8,64,256]{2,1,0:T(8,128)(2,1)S(1)} %bitcast.22), channel_id=1, replica_groups=mesh['x'=4,'c'=2,'z'=8,'y'=4] {'z'}, dimensions={0} | all-to-all | bytes 524288 | tf_op jit(solution)/shard_map/all_to_all | solution.py:121
  96.4 12.9 %all_to_all.69 = bf16[8,64,256]{2,1,0:T(8,128)(2,1)S(1)} all-to-all(bf16[8,64,256]{2,1,0:T(8,128)(2,1)S(1)} %broadcast_in_dim.7), channel_id=1, replica_groups=mesh['x'=4,'c'=2,'z'=8,'y'=4] {'z'}, dimensions={0} | all-to-all | bytes 524288 | tf_op jit(solution)/shard_map/all_to_all | solution.py:123
  109.2 3.9 %shard_map.71 = (bf16[4,128,1024]{2,1,0:T(8,128)(2,1)}, bf16[4,256,1024]{2,1,0:T(8,128)(2,1)S(1)}) custom-call(s32[4,8]{1,0:T(4,128)S(1)} %copy-done.4, bf16[512,256]{1,0:T(8,128)(2,1)S(1)} %bitcast.19, bf16[8,64,32,128]{3,2,1,0:T(8,128)(2,1)} %bitcast.25), custom_call_target="tpu_custom_call" | custom-call | tf_op jit(solution)/shard_map/pallas_call | solution.py:187
  113.2 1.3 copy-done.2
  114.5 3.5 %all-to-all-start.5 = ((bf16[4,128,1024]{2,1,0:T(8,128)(2,1)}), bf16[4,128,1024]{2,1,0:T(8,128)(2,1)S(1)}, u32[]{:S(2)}, u32[]{:S(2)}) async-start(bf16[4,128,1024]{2,1,0:T(8,128)(2,1)} %get-tuple-element.10), calls=%async_computation.5 | async-start | bytes 2097152 | tf_op jit(solution)/shard_map/all_to_all | solution.py:190
  118.0 0.0 reduce-scatter.5.cloned.1.call-start
  118.1 0.0 copy-done.6
  118.1 0.1 copy.7.weight_ref
  118.3 11.7 %all-to-all-done.5.recon_ref = bf16[4,128,1024]{2,1,0:T(8,128)(2,1)S(1)} async-done(((bf16[4,128,1024]{2,1,0:T(8,128)(2,1)}), bf16[4,128,1024]{2,1,0:T(8,128)(2,1)S(1)}, u32[]{:S(2)}, u32[]{:S(2)}) %all-to-all-start.5) | async-done | bytes 1048608 | tf_op jit(solution)/shard_map/all_to_all | solution.py:190
  130.0 0.2 shard_map.72
  130.2 13.4 %all_to_all.70.gout_ref = bf16[4,128,1024]{2,1,0:T(8,128)(2,1)S(1)} all-to-all(bf16[4,128,1024]{2,1,0:T(8,128)(2,1)S(1)} %shard_map.72), channel_id=1, replica_groups=mesh['x'=4,'c'=2,'z'=8,'y'=4] {'y'}, dimensions={0} | all-to-all | bytes 2097152 | tf_op jit(solution)/shard_map/all_to_all | solution.py:192
  143.6 0.0 copy-done.3
  143.6 5.7 %shard_map.73 = (bf16[512,256]{1,0:T(8,128)(2,1)S(1)}, bf16[8,64,32,128]{3,2,1,0:T(8,128)(2,1)}) custom-call(s32[4,8]{1,0:T(4,128)S(1)} %copy-done.4, bf16[512,256]{1,0:T(8,128)(2,1)S(1)} %bitcast.20, bf16[4,128,1024]{2,1,0:T(8,128)(2,1)S(1)} %all_to_all.70.gout_ref, bf16[4,256,1024]{2,1,0:T(8,128)(2,1)S(1)} %copy-done.3), custom_call_target="tpu_custom_call" | custom-call | tf_op jit(solution)/shard_map/pallas_call | solution.py:193
  149.3 0.0 reduce-scatter.5.cloned.1.call-update
  149.3 0.0 reduce-scatter.3.cloned.1.call-start
  149.3 21.1 %all_to_all.71 = bf16[8,64,256]{2,1,0:T(8,128)(2,1)S(1)} all-to-all(bf16[8,64,256]{2,1,0:T(8,128)(2,1)S(1)} %bitcast.23), channel_id=1, replica_groups=mesh['x'=4,'c'=2,'z'=8,'y'=4] {'z'}, dimensions={0} | all-to-all | bytes 524288 | tf_op jit(solution)/shard_map/all_to_all | solution.py:121
  170.5 12.9 %all_to_all.72 = bf16[8,64,256]{2,1,0:T(8,128)(2,1)S(1)} all-to-all(bf16[8,64,256]{2,1,0:T(8,128)(2,1)S(1)} %broadcast_in_dim.8), channel_id=1, replica_groups=mesh['x'=4,'c'=2,'z'=8,'y'=4] {'z'}, dimensions={0} | all-to-all | bytes 524288 | tf_op jit(solution)/shard_map/all_to_all | solution.py:123
  183.3 2.9 %shard_map.74 = bf16[8,64,32,128]{3,2,1,0:T(8,128)(2,1)S(1)} custom-call(s32[4,8]{1,0:T(4,128)S(1)} %copy-done.4, bf16[512,256]{1,0:T(8,128)(2,1)S(1)} %bitcast.21, bf16[4,512,256]{2,1,0:T(8,128)(2,1)S(1)} %all_to_all.67.tok_ref), custom_call_target="tpu_custom_call" | custom-call | tf_op jit(solution)/shard_map/pallas_call | solution.py:198
  186.3 0.0 copy-start
  186.3 1.9 copy-done
  188.2 0.0 reduce-scatter.3.cloned.1.call-update
  188.2 1.1 reduce-scatter.5.cloned.1.call-done
  189.4 27.9 %all_to_all.73 = bf16[32,2,32,128]{3,2,1,0:T(8,128)(2,1)} all-to-all(bf16[32,2,32,128]{3,2,1,0:T(8,128)(2,1)} %bitcast.28), channel_id=1, replica_groups=mesh['x'=4,'c'=2,'z'=8,'y'=4] {'z','y'}, dimensions={0} | all-to-all | bytes 1048576 | tf_op jit(solution)/shard_map/all_to_all | solution.py:166
  217.2 5.4 %all-to-all-start.12 = ((bf16[8,4,2,32,128]{4,3,2,1,0:T(8,128)(2,1)}), bf16[8,4,2,32,128]{4,3,2,1,0:T(8,128)(2,1)S(1)}, u32[]{:S(2)}, u32[]{:S(2)}) async-start(bf16[8,4,2,32,128]{4,3,2,1,0:T(8,128)(2,1)} %bitcast.16), calls=%async_computation.14 | async-start | bytes 1048576 | tf_op jit(solution)/shard_map/all_to_all | solution.py:167
  222.6 13.2 %reduce-scatter.3.cloned.1.call-done = bf16[2048,128]{1,0:T(8,128)(2,1)} async-done(((bf16[16384,128]{1,0:T(8,128)(2,1)}), bf16[2048,128]{1,0:T(8,128)(2,1)}) %reduce-scatter.3.cloned.1.call-update) | async-done | bytes 524304 | tf_op jit(solution)/shard_map/reduce_scatter | solution.py:165
  235.8 0.0 all-to-all-done.12.in_ref
  235.8 28.4 %all_to_all.74 = bf16[32,2,32,128]{3,2,1,0:T(8,128)(2,1)} all-to-all(bf16[32,2,32,128]{3,2,1,0:T(8,128)(2,1)} %bitcast.29), channel_id=1, replica_groups=mesh['x'=4,'c'=2,'z'=8,'y'=4] {'z','y'}, dimensions={0} | all-to-all | bytes 1048576 | tf_op jit(solution)/shard_map/all_to_all | solution.py:166
  264.2 5.2 %all-to-all-start.10 = ((bf16[8,4,2,32,128]{4,3,2,1,0:T(8,128)(2,1)}), bf16[8,4,2,32,128]{4,3,2,1,0:T(8,128)(2,1)S(1)}, u32[]{:S(2)}, u32[]{:S(2)}) async-start(bf16[8,4,2,32,128]{4,3,2,1,0:T(8,128)(2,1)} %bitcast.13), calls=%async_computation.11 | async-start | bytes 1048576 | tf_op jit(solution)/shard_map/all_to_all | solution.py:167
  269.4 1.1 shard_map.76
  270.5 7.8 %all-to-all-done.10.in_ref = bf16[8,4,2,32,128]{4,3,2,1,0:T(8,128)(2,1)S(1)} async-done(((bf16[8,4,2,32,128]{4,3,2,1,0:T(8,128)(2,1)}), bf16[8,4,2,32,128]{4,3,2,1,0:T(8,128)(2,1)S(1)}, u32[]{:S(2)}, u32[]{:S(2)}) %all-to-all-start.10) | async-done | bytes 524320 | tf_op jit(solution)/shard_map/all_to_all | solution.py:167
  278.3 1.1 shard_map.75
  (10 shorter events, 0.1 us)
Async XLA Ops:
  7.2 71.6 %all-gather.3.cloned.1.call-start = ((), (), s32[]{:S(2)}) async-start(), calls=%async_computation.15 | async-start | bytes 4718592 | tf_op jit(solution)/shard_map/all_gather | solution.py:161
  38.5 23.9 %copy-start.5 = (bf16[512,256]{1,0:T(8,128)(2,1)S(1)}, bf16[512,256]{1,0:T(8,128)(2,1)}, u32[]{:S(2)}) copy-start(bf16[512,256]{1,0:T(8,128)(2,1)} %param.5) | copy-start | bytes 786436
  38.5 70.8 %all-gather.5.cloned.1.call-start = ((), (), s32[]{:S(2)}) async-start(), calls=%async_computation.16 | async-start | bytes 4718592 | tf_op jit(solution)/shard_map/all_gather | solution.py:161
  40.5 38.3 %copy-start.4 = (s32[4,8]{1,0:T(4,128)S(1)}, s32[4,8]{1,0:T(4,128)}, u32[]{:S(2)}) copy-start(s32[4,8]{1,0:T(4,128)} %ids_ref.7) | copy-start | bytes 388
  78.8 2.2 copy-start.1
  82.4 35.7 %copy-start.6 = (s32[512]{0:T(512)S(1)}, s32[512]{0:T(512)}, u32[]{:S(2)}) copy-start(s32[512]{0:T(512)} %param.9) | copy-start | bytes 6148
  113.2 1.3 copy-start.2
  114.5 15.5 %all-to-all-start.5 = ((bf16[4,128,1024]{2,1,0:T(8,128)(2,1)}), bf16[4,128,1024]{2,1,0:T(8,128)(2,1)S(1)}, u32[]{:S(2)}, u32[]{:S(2)}) async-start(bf16[4,128,1024]{2,1,0:T(8,128)(2,1)} %get-tuple-element.10), calls=%async_computation.5 | async-start | bytes 2097152 | tf_op jit(solution)/shard_map/all_to_all | solution.py:190
  118.0 71.3 %reduce-scatter.5.cloned.1.call-start = ((), (), s32[]{:S(2)}) async-start(), calls=%async_computation.18 | async-start | bytes 4718592 | tf_op jit(solution)/shard_map/reduce_scatter | solution.py:165
  130.0 13.6 %copy-start.3 = (bf16[4,256,1024]{2,1,0:T(8,128)(2,1)S(1)}, bf16[4,256,1024]{2,1,0:T(8,128)(2,1)}, u32[]{:S(2)}) copy-start(bf16[4,256,1024]{2,1,0:T(8,128)(2,1)} %copy-done.2) | copy-start | bytes 6291460
  149.3 86.5 %reduce-scatter.3.cloned.1.call-start = ((), (), s32[]{:S(2)}) async-start(), calls=%async_computation.17 | async-start | bytes 4718592 | tf_op jit(solution)/shard_map/reduce_scatter | solution.py:165
  186.3 2.0 copy-start
  217.2 18.6 %all-to-all-start.12 = ((bf16[8,4,2,32,128]{4,3,2,1,0:T(8,128)(2,1)}), bf16[8,4,2,32,128]{4,3,2,1,0:T(8,128)(2,1)S(1)}, u32[]{:S(2)}, u32[]{:S(2)}) async-start(bf16[8,4,2,32,128]{4,3,2,1,0:T(8,128)(2,1)} %bitcast.16), calls=%async_computation.14 | async-start | bytes 1048576 | tf_op jit(solution)/shard_map/all_to_all | solution.py:167
  264.2 14.1 %all-to-all-start.10 = ((bf16[8,4,2,32,128]{4,3,2,1,0:T(8,128)(2,1)}), bf16[8,4,2,32,128]{4,3,2,1,0:T(8,128)(2,1)S(1)}, u32[]{:S(2)}, u32[]{:S(2)}) async-start(bf16[8,4,2,32,128]{4,3,2,1,0:T(8,128)(2,1)} %bitcast.13), calls=%async_computation.11 | async-start | bytes 1048576 | tf_op jit(solution)/shard_map/all_to_all | solution.py:167
Sparse Core Ops, SparseCore 0:
  38.6 29.7 all-gather.2
  70.3 34.6 all-gather.4
  149.4 39.8 reduce-scatter.4
  191.8 44.0 reduce-scatter.2

commit v5 on v4

v5 whole, which is shorter than its diff:
```python
import functools

import jax
import jax.numpy as jnp
import numpy as np
from jax import lax
from jax.experimental import pallas as pl
from jax.experimental.pallas import tpu as pltpu
from jax.sharding import Mesh
from jax.sharding import PartitionSpec as P

BLOCK = 128
VMEM = pltpu.CompilerParams(vmem_limit_bytes=48 * 1024 * 1024)
ALL_VMEM = pltpu.CompilerParams(vmem_limit_bytes=61 * 1024 * 1024)
NT = (((1,), (1,)), ((), ()))
TN = (((0,), (0,)), ((), ()))
SMEM_SPEC = pl.BlockSpec(memory_space=pltpu.SMEM)
VMEM_SPEC = pl.BlockSpec(memory_space=pltpu.VMEM)


def dot(left, right, dims):
    return lax.dot_general(left, right, dims, preferred_element_type=jnp.float32)


def split_kernel(nh, nl, ny, sub, lanes, d_ref, in_ref, out_ref):
    for h in range(nh):
        for l in range(nl):
            for i in range(in_ref.shape[0] // BLOCK):
                at = i * BLOCK + h * sub
                for q in range(ny):
                    col = (q * nl + l) * lanes
                    out_ref[h * nl + l, i, :, q * lanes : (q + 1) * lanes] = in_ref[at : at + sub, col : col + lanes]


def select(ids_ref, weight_ref, t, act, sel_ref):
    pieces, _, sub, lanes = weight_ref.shape
    for a in range(act):
        for p in range(pieces):
            sel_ref[t, a * sub : (a + 1) * sub, p * lanes : (p + 1) * lanes] = weight_ref[p, ids_ref[t, a]]


def token_rows(tok_ref, at):
    quarters, pieces = tok_ref.shape[:2]
    return jnp.concatenate([tok_ref[q, p, at, :] for p in range(pieces) for q in range(quarters)], axis=1)


def block(t):
    return slice(t * BLOCK, (t + 1) * BLOCK)


def pre_kernel(tb, act, ids_ref, tok_ref, enc_ref, out_ref, sel_ref):
    for t in range(tb):
        select(ids_ref, enc_ref, t, act, sel_ref)
        out_ref[block(t), :] = dot(token_rows(tok_ref, block(t)), sel_ref[t], NT).astype(jnp.bfloat16)


def recon_kernel(tb, act, ids_ref, codes_ref, dec_ref, out_ref, sel_ref):
    for t in range(tb):
        select(ids_ref, dec_ref, t, act, sel_ref)
        out_ref[t] = jnp.dot(
            codes_ref[block(t), :], sel_ref[t], preferred_element_type=jnp.float32
        ).astype(jnp.bfloat16)


def error_kernel(mine_ref, tok_ref, weight_ref, recon_ref, out_ref):
    at = pl.ds(pl.multiple_of(mine_ref[0] * BLOCK, BLOCK), BLOCK)
    recon = recon_ref[0].astype(jnp.float32)
    for k in range(1, recon_ref.shape[0]):
        recon += recon_ref[k].astype(jnp.float32)
    gout = weight_ref[at, :] * (recon - token_rows(tok_ref, at).astype(jnp.float32))
    gout = gout.astype(jnp.bfloat16)
    for k in range(out_ref.shape[0]):
        out_ref[k] = gout


def sum_rows(tb, act, ids_ref, codes_ref, rows_of, prod_ref, acc_ref, out_ref):
    pieces, blocks, sub, lanes = acc_ref.shape
    acc_ref[...] = jnp.zeros_like(acc_ref)
    for t in range(tb):
        prod_ref[...] = dot(codes_ref[block(t), :], rows_of(t), TN)
        for a in range(act):
            for p in range(pieces):
                acc_ref[p, ids_ref[t, a]] += prod_ref[a * sub : (a + 1) * sub, p * lanes : (p + 1) * lanes]

    @pl.loop(0, blocks)
    def _(b):
        for p in range(pieces):
            out_ref[p, b] = acc_ref[p, b].astype(jnp.bfloat16)


def dec_kernel(tb, act, ids_ref, codes_ref, gout_ref, sel_ref, part_ref, grad_ref, prod_ref, acc_ref):
    for t in range(tb):
        part_ref[block(t), :] = dot(gout_ref[t], sel_ref[t], NT).astype(jnp.bfloat16)
    sum_rows(tb, act, ids_ref, codes_ref, lambda t: gout_ref[t], prod_ref, acc_ref, grad_ref)


def enc_kernel(tb, act, ids_ref, codes_ref, tok_ref, grad_ref, prod_ref, acc_ref):
    sum_rows(tb, act, ids_ref, codes_ref, lambda t: token_rows(tok_ref, block(t)), prod_ref, acc_ref, grad_ref)


def join_kernel(nh, nl, ny, lanes, in_ref, out_ref):
    _, blocks, sub, _ = in_ref.shape
    for h in range(nh):
        for l in range(nl):
            for i in range(blocks):
                at = i * BLOCK + h * sub
                for q in range(ny):
                    col = (q * nl + l) * lanes
                    part = in_ref[h * nl + l, i, :, q * lanes : (q + 1) * lanes]
                    out_ref[at : at + sub, col : col + lanes] = part.astype(jnp.float32)


def call(kernel, out_shape, n_smem, n_vmem, scratch=()):
    many = isinstance(out_shape, tuple)
    return pl.pallas_call(
        kernel,
        out_shape=out_shape,
        in_specs=[SMEM_SPEC] * n_smem + [VMEM_SPEC] * n_vmem,
        out_specs=(VMEM_SPEC,) * len(out_shape) if many else VMEM_SPEC,
        scratch_shapes=list(scratch),
        compiler_params=VMEM,
    )


def all_sum(part, axis, n):
    got = lax.all_to_all(part.reshape(n, -1, part.shape[1]), axis, 0, 0, tiled=True)
    mine = jnp.sum(got.astype(jnp.float32), axis=0).astype(part.dtype)
    got = lax.all_to_all(jnp.broadcast_to(mine[None], got.shape), axis, 0, 0, tiled=True)
    return got.reshape(part.shape)


def per_device(tokens, enc_weight, dec_weight, active_blocks, counts, *, sizes):
    nx, nc, nh, nl, ny = (sizes[k] for k in ("x", "c", "h", "l", "y"))
    group, feat, inner = ("c", "y"), ("x", "l"), ("h", "l")
    tok_dev, width = tokens.shape
    tb, act = active_blocks.shape
    rows, model = enc_weight.shape
    feats = model // (nx * nl)
    lanes = width // nl
    cols = feats // nc
    sub = BLOCK // nh
    own_blocks = rows // BLOCK
    blocks = nh * nl * ny * own_blocks
    d = lax.axis_index(("x", "c")).astype(jnp.int32).reshape(1)
    h = lax.axis_index("h").astype(jnp.int32).reshape(1)

    def spread(weight):
        out = (nh * nl, own_blocks, sub, cols)
        pieces = pl.pallas_call(
            functools.partial(split_kernel, nh, nl, ny, sub, lanes),
            out_shape=jax.ShapeDtypeStruct(out, jnp.bfloat16),
            grid_spec=pltpu.PrefetchScalarGridSpec(
                num_scalar_prefetch=1,
                grid=(1,),
                in_specs=[pl.BlockSpec((rows, nc * cols), lambda i, d_ref: (0, d_ref[0]))],
                out_specs=pl.BlockSpec(out, lambda i, d_ref: (0, 0, 0, 0)),
            ),
            compiler_params=ALL_VMEM,
        )(d, weight)
        return lax.all_to_all(pieces, inner, 0, 0, tiled=True)

    def gather(pieces):
        whole = lax.all_gather(pieces.reshape(-1, cols), group, axis=0, tiled=True)
        return whole.reshape(nc, blocks, sub, cols)

    def own(grad):
        part = lax.psum_scatter(grad.reshape(-1, cols), group, scatter_dimension=0, tiled=True)
        part = lax.all_to_all(part.reshape(nh * nl, own_blocks, sub, cols), inner, 0, 0, tiled=True)
        return call(
            functools.partial(join_kernel, nh, nl, ny, lanes),
            jax.ShapeDtypeStruct((rows, nc * cols), jnp.float32),
            0,
            1,
        )(part)

    swap = [
        ((x * nh + g) * ny + q, (g * nh + q) * ny + x) for x in range(nx) for g in range(nh) for q in range(ny)
    ]
    small = jnp.concatenate([counts, active_blocks.reshape(-1)])
    small = lax.ppermute(small, ("x", "h", "y"), swap)
    tokens = lax.ppermute(tokens, ("x", "h", "y"), swap)
    mine, tokens, small = lax.optimization_barrier((spread(enc_weight), tokens, small))
    enc = gather(mine)
    dec_weight, tokens, mine = lax.optimization_barrier((dec_weight, tokens, mine))
    dec = gather(spread(dec_weight))
    weights = small[:tok_dev].astype(jnp.float32)[:, None] / BLOCK
    ids = small[tok_dev:].reshape(tb, act)
    ids = (ids // own_blocks % ny * (nh * nl) + ids // (own_blocks * ny)) * own_blocks + ids % own_blocks
    parts = jnp.stack([tokens[:, l * lanes : (l + 1) * lanes] for l in range(nl)])
    parts = jnp.broadcast_to(parts[None], (nh, *parts.shape)).reshape(nh * nl, tok_dev, lanes)
    tok = lax.all_to_all(parts, inner, 0, 0, tiled=True).reshape(nh, nl, tok_dev, lanes)

    half = jnp.bfloat16
    codes_like = jax.ShapeDtypeStruct((tok_dev, act * sub), half)
    sel_like = jax.ShapeDtypeStruct((tb, act * sub, feats), half)
    rows_like = jax.ShapeDtypeStruct((tb, BLOCK, feats), half)
    grad_like = jax.ShapeDtypeStruct((nc, blocks, sub, cols), half)
    sums = (pltpu.VMEM((act * sub, feats), jnp.float32), pltpu.VMEM((nc, blocks, sub, cols), jnp.float32))

    part = call(
        functools.partial(pre_kernel, tb, act), codes_like, 1, 2, [pltpu.VMEM(sel_like.shape, half)]
    )(ids, tok, enc)
    codes = all_sum(part, feat, nx * nl)
    recon, sel = call(functools.partial(recon_kernel, tb, act), (rows_like, sel_like), 1, 2)(
        ids, codes, dec
    )
    recon = lax.all_to_all(recon, "h", 0, 0, tiled=True)
    gout = call(error_kernel, rows_like, 1, 3)(h, tok, weights, recon)
    gout = lax.all_to_all(gout, "h", 0, 0, tiled=True)
    part, group_dec = call(functools.partial(dec_kernel, tb, act), (codes_like, grad_like), 1, 3, sums)(
        ids, codes, gout, sel
    )
    grad_dec = own(group_dec)
    grad_codes = all_sum(part, feat, nx * nl)
    group_enc = call(functools.partial(enc_kernel, tb, act), grad_like, 1, 2, sums)(
        ids, grad_codes, tok
    )
    grad_enc = own(group_enc)
    return (grad_enc, grad_dec)


def solution(mesh):
    fine = Mesh(np.asarray(mesh.devices).reshape(4, 2, 4, 2, 4), ("x", "c", "h", "l", "y"))
    dp, latent = ("x", "c"), ("h", "l", "y")
    return jax.shard_map(
        functools.partial(per_device, sizes=dict(fine.shape)),
        mesh=fine,
        in_specs=(P(dp, latent), P(latent, None), P(latent, None), P(dp, None), P(dp)),
        out_specs=(P(latent, dp), P(latent, dp)),
        check_vma=False,
    )
```

time: 289 us -> 342 us (1.18)
  waiting for transfers between devices: 33.9 us -> 152 us
  blocking collectives: 198 us -> 110 us
  starting transfers between devices: 14.3 us -> 35.9 us
    all_to_all x6 -> x3, blocking collectives: 137 us -> 81.2 us  [the longest x1 29.5 us: per_device(): gout = lax.all_to_all(gout, 'h', 0, 0, tiled=True)]
    all_to_all x3 -> x5, waiting for transfers between devices: 19.5 us -> 70 us  [the longest x1 25.5 us: per_device(): lax.all_to_all(parts, inner, 0, 0, tiled=True)]
    reduce_scatter x2, waiting for transfers between devices: 14.3 us -> 58.8 us  [own(): lax.psum_scatter(grad.reshape(-1, cols), group, scatter_dimension=0, tile...]
    ppermute x0 -> x2, waiting for transfers between devices: none -> 23.4 us  [the longest x1 23.4 us: per_device(): small = lax.ppermute(small, ('x', 'h', 'y'), swap)]
    all_to_all x2 -> x1, blocking collectives: 25.8 us -> 9.82 us  [all_sum(): lax.all_to_all(jnp.broadcast_to(mine[None], got.shape), axis, 0, 0, tiled...]
    all_to_all x2, blocking collectives: 34.9 us -> 19.1 us  [all_sum(): lax.all_to_all(part.reshape(n, -1, part.shape[1]), axis, 0, 0, tiled=True)]
    all_to_all x3 -> x5, starting transfers between devices: 14.1 us -> 27.7 us  [the longest x1 8.47 us: spread(): return lax.all_to_all(pieces, inner, 0, 0, tiled=True)]
    ppermute x0 -> x2, starting transfers between devices: none -> 8.13 us  [the longest x1 4.67 us: per_device(): small = lax.ppermute(small, ('x', 'h', 'y'), swap)]
  transfers between devices with their start and end apart: 7 -> 11, of which waited for: 4 -> 7; matrix products, arithmetic and copies ran while one was open for 0% -> 1% of each run, Pallas kernels for 3% -> 2%
where the time goes in v5:
time: 342 us; the launch traced here: 340 us
  waiting for transfers between devices  152 us (44%)
  blocking collectives  110 us (32%)
  starting transfers between devices  35.9 us (10%)
  Pallas kernels  18.8 us (5%)
  between operations  14 us (4%)
  local copies, waits for them, and re-layouts  8.58 us (3%)
    reduce_scatter x2, waiting for transfers between devices, own(): lax.psum_scatter(grad.reshape(-1, cols), group, scatter_dimension=0, tile...  58.8 us
    all_to_all x1, blocking collectives, per_device(): gout = lax.all_to_all(gout, 'h', 0, 0, tiled=True)  29.5 us
    all_to_all x1, blocking collectives, spread(): return lax.all_to_all(pieces, inner, 0, 0, tiled=True)  26.9 us
    all_to_all x1, waiting for transfers between devices, per_device(): lax.all_to_all(parts, inner, 0, 0, tiled=True)  25.5 us
    all_to_all x1, blocking collectives, own(): lax.all_to_all(part.reshape(nh * nl, own_blocks, sub, cols), inner, 0, 0,...  24.8 us
    ppermute x1, waiting for transfers between devices, per_device(): small = lax.ppermute(small, ('x', 'h', 'y'), swap)  23.4 us
    all_to_all x1, waiting for transfers between devices, per_device(): recon = lax.all_to_all(recon, 'h', 0, 0, tiled=True)  22.2 us
    all_to_all x2, blocking collectives, all_sum(): lax.all_to_all(part.reshape(n, -1, part.shape[1]), axis, 0, 0, tiled=True)  19.1 us
  transfers between devices with their start and end apart: 11, of which 7 were waited for; matrix products, arithmetic and copies ran while one was open for 1% of the time, Pallas kernels for 2%

profile of v5, /device:TPU:2, one launch (start us, length us, event | category | flops | bytes accessed | tf_op | source)
XLA Modules:
  0.0 339.8 jit_solution(783851674816696235)
XLA Ops:
  7.2 2.0 shard_map.68
  9.2 8.5 %all-to-all-start = ((bf16[8,2,32,512]{3,2,1,0:T(8,128)(2,1)}), bf16[8,2,32,512]{3,2,1,0:T(8,128)(2,1)S(1)}, u32[]{:S(2)}, u32[]{:S(2)}) async-start(bf16[8,2,32,512]{3,2,1,0:T(8,128)(2,1)} %shard_map.68), calls=%async_computation | async-start | bytes 1048576 | tf_op jit(solution)/shard_map/all_to_all | solution.py:160
  17.6 0.0 all-gather.3.cloned.1.call-start
  17.7 3.5 %collective-permute-start = (bf16[512,256]{1,0:T(8,128)(2,1)S(1)}, bf16[512,256]{1,0:T(8,128)(2,1)S(1)}, u32[]{:S(2)}, u32[]{:S(2)}) collective-permute-start(bf16[512,256]{1,0:T(8,128)(2,1)S(1)} %copy-done.7), channel_id=1, source_target_pairs={{0,0},{1,8},{2,16},{3,24},{8,64},{9,72},{10,80},{11,88},{16,128},{... | collective-permute-start | bytes 786440 | tf_op jit(solution)/shard_map/ppermute | solution.py:181
  21.2 0.1 reshape.71
  21.3 4.7 %collective-permute-start.1 = (s32[544]{0:T(1024)S(1)}, s32[544]{0:T(1024)S(1)}, u32[]{:S(2)}, u32[]{:S(2)}) collective-permute-start(s32[544]{0:T(1024)S(1)} %pad_add_fusion), channel_id=1, source_target_pairs={{0,0},{1,8},{2,16},{3,24},{8,64},{9,72},{10,80},{11,88},{16,128},{... | collective-permute-start | bytes 6536 | tf_op jit(solution)/shard_map/ppermute | solution.py:180
  25.9 23.4 %collective-permute-done.1 = s32[544]{0:T(1024)S(1)} collective-permute-done((s32[544]{0:T(1024)S(1)}, s32[544]{0:T(1024)S(1)}, u32[]{:S(2)}, u32[]{:S(2)}) %collective-permute-start.1) | collective-permute-done | bytes 2208 | tf_op jit(solution)/shard_map/ppermute | solution.py:180
  49.4 0.0 collective-permute-done
  49.4 0.0 all-to-all-done
  49.4 0.8 copy-done.4
  50.2 0.0 all-gather.3.cloned.1.call-update
  50.2 0.0 all-gather.5.cloned.1.call-start
  50.2 1.9 shard_map.70
  52.2 26.9 %all_to_all.55 = bf16[8,2,32,512]{3,2,1,0:T(8,128)(2,1)} all-to-all(bf16[8,2,32,512]{3,2,1,0:T(8,128)(2,1)} %shard_map.70), channel_id=1, replica_groups=mesh['x'=4,'c'=2,'h'=4,'l'=2,'y'=4] {'h','l'}, dimensions={0} | all-to-all | bytes 1048576 | tf_op jit(solution)/shard_map/all_to_all | solution.py:160
  79.1 0.0 all-gather.5.cloned.1.call-update
  79.2 1.1 broadcast_in_dim.6
  80.3 3.6 %all-to-all-start.1 = ((bf16[8,512,128]{2,1,0:T(8,128)(2,1)}), bf16[8,512,128]{2,1,0:T(8,128)(2,1)S(1)}, u32[]{:S(2)}, u32[]{:S(2)}) async-start(bf16[8,512,128]{2,1,0:T(8,128)(2,1)} %bitcast.3), calls=%async_computation.1 | async-start | bytes 2097152 | tf_op jit(solution)/shard_map/all_to_all | solution.py:191
  83.8 0.1 reshape.72
  84.0 25.5 %all-to-all-done.1 = bf16[8,512,128]{2,1,0:T(8,128)(2,1)S(1)} async-done(((bf16[8,512,128]{2,1,0:T(8,128)(2,1)}), bf16[8,512,128]{2,1,0:T(8,128)(2,1)S(1)}, u32[]{:S(2)}, u32[]{:S(2)}) %all-to-all-start.1) | async-done | bytes 1048608 | tf_op jit(solution)/shard_map/all_to_all | solution.py:191
  109.5 2.3 copy-done.1
  111.7 1.4 shard_map.69
  113.1 8.6 %all_to_all.56 = bf16[8,64,256]{2,1,0:T(8,128)(2,1)S(1)} all-to-all(bf16[8,64,256]{2,1,0:T(8,128)(2,1)S(1)} %bitcast.29), channel_id=1, replica_groups=mesh['x'=4,'c'=2,'h'=4,'l'=2,'y'=4] {'x','l'}, dimensions={0} | all-to-all | bytes 524288 | tf_op jit(solution)/shard_map/all_to_all | solution.py:126
  121.8 0.7 broadcast_in_dim.7
  122.5 5.1 %all-to-all-start.3 = ((bf16[8,64,256]{2,1,0:T(8,128)(2,1)}), bf16[8,64,256]{2,1,0:T(8,128)(2,1)S(1)}, u32[]{:S(2)}, u32[]{:S(2)}) async-start(bf16[8,64,256]{2,1,0:T(8,128)(2,1)} %broadcast_in_dim.7), calls=%async_computation.3 | async-start | bytes 524288 | tf_op jit(solution)/shard_map/all_to_all | solution.py:128
  127.6 5.5 %all-to-all-done.3 = bf16[8,64,256]{2,1,0:T(8,128)(2,1)S(1)} async-done(((bf16[8,64,256]{2,1,0:T(8,128)(2,1)}), bf16[8,64,256]{2,1,0:T(8,128)(2,1)S(1)}, u32[]{:S(2)}, u32[]{:S(2)}) %all-to-all-start.3) | async-done | bytes 262176 | tf_op jit(solution)/shard_map/all_to_all | solution.py:128
  133.1 3.7 %shard_map.71 = (bf16[4,128,1024]{2,1,0:T(8,128)(2,1)}, bf16[4,256,1024]{2,1,0:T(8,128)(2,1)S(1)}) custom-call(s32[4,8]{1,0:T(4,128)S(1)} %fusion.4.ids_ref, bf16[512,256]{1,0:T(8,128)(2,1)S(1)} %bitcast.26, bf16[2,64,32,512]{3,2,1,0:T(8,128)(2,1)} %bitcast.31), custom_call_target="tpu_custom_call" | custom-call | tf_op jit(solution)/shard_map/pallas_call | solution.py:204
  136.8 1.3 copy-done.2
  138.1 3.5 %all-to-all-start.5 = ((bf16[4,128,1024]{2,1,0:T(8,128)(2,1)}), bf16[4,128,1024]{2,1,0:T(8,128)(2,1)S(1)}, u32[]{:S(2)}, u32[]{:S(2)}) async-start(bf16[4,128,1024]{2,1,0:T(8,128)(2,1)} %get-tuple-element.16), calls=%async_computation.5 | async-start | bytes 2097152 | tf_op jit(solution)/shard_map/all_to_all | solution.py:207
  141.7 0.0 reduce-scatter.5.cloned.1.call-start
  141.7 0.1 copy.7.weight_ref
  141.9 22.2 %all-to-all-done.5.recon_ref = bf16[4,128,1024]{2,1,0:T(8,128)(2,1)S(1)} async-done(((bf16[4,128,1024]{2,1,0:T(8,128)(2,1)}), bf16[4,128,1024]{2,1,0:T(8,128)(2,1)S(1)}, u32[]{:S(2)}, u32[]{:S(2)}) %all-to-all-start.5) | async-done | bytes 1048608 | tf_op jit(solution)/shard_map/all_to_all | solution.py:207
  164.1 0.2 shard_map.72
  164.3 29.5 %all_to_all.57.gout_ref = bf16[4,128,1024]{2,1,0:T(8,128)(2,1)S(1)} all-to-all(bf16[4,128,1024]{2,1,0:T(8,128)(2,1)S(1)} %shard_map.72), channel_id=1, replica_groups=mesh['x'=4,'c'=2,'h'=4,'l'=2,'y'=4] {'h'}, dimensions={0} | all-to-all | bytes 2097152 | tf_op jit(solution)/shard_map/all_to_all | solution.py:209
  193.8 5.1 %shard_map.73 = (bf16[512,256]{1,0:T(8,128)(2,1)S(1)}, bf16[2,64,32,512]{3,2,1,0:T(8,128)(2,1)}) custom-call(s32[4,8]{1,0:T(4,128)S(1)} %fusion.4.ids_ref, bf16[512,256]{1,0:T(8,128)(2,1)S(1)} %bitcast.27, bf16[4,128,1024]{2,1,0:T(8,128)(2,1)S(1)} %all_to_all.57.gout_ref, bf16[4,256,1024]{2,1,0:T(8,128)(2,1)S(1)} %copy-done.3), custom_call_target="tpu_custom_call" | custom-call | tf_op jit(solution)/shard_map/pallas_call | solution.py:210
  199.0 0.0 reduce-scatter.5.cloned.1.call-update
  199.0 0.0 reduce-scatter.3.cloned.1.call-start
  199.0 10.5 %all_to_all.58 = bf16[8,64,256]{2,1,0:T(8,128)(2,1)S(1)} all-to-all(bf16[8,64,256]{2,1,0:T(8,128)(2,1)S(1)} %bitcast.30), channel_id=1, replica_groups=mesh['x'=4,'c'=2,'h'=4,'l'=2,'y'=4] {'x','l'}, dimensions={0} | all-to-all | bytes 524288 | tf_op jit(solution)/shard_map/all_to_all | solution.py:126
  209.6 9.8 %all_to_all.59 = bf16[8,64,256]{2,1,0:T(8,128)(2,1)S(1)} all-to-all(bf16[8,64,256]{2,1,0:T(8,128)(2,1)S(1)} %broadcast_in_dim.8), channel_id=1, replica_groups=mesh['x'=4,'c'=2,'h'=4,'l'=2,'y'=4] {'x','l'}, dimensions={0} | all-to-all | bytes 524288 | tf_op jit(solution)/shard_map/all_to_all | solution.py:128
  219.4 2.4 shard_map.74
  221.8 2.0 copy-done
  223.8 0.0 reduce-scatter.3.cloned.1.call-update
  223.8 26.7 %reduce-scatter.5.cloned.1.call-done = bf16[512,512]{1,0:T(8,128)(2,1)} async-done(((bf16[4096,512]{1,0:T(8,128)(2,1)}), bf16[512,512]{1,0:T(8,128)(2,1)}) %reduce-scatter.5.cloned.1.call-update) | async-done | bytes 524304 | tf_op jit(solution)/shard_map/reduce_scatter | solution.py:167
  250.5 24.8 %all_to_all.60.in_ref = bf16[8,2,32,512]{3,2,1,0:T(8,128)(2,1)S(1)} all-to-all(bf16[8,2,32,512]{3,2,1,0:T(8,128)(2,1)} %bitcast.35), channel_id=1, replica_groups=mesh['x'=4,'c'=2,'h'=4,'l'=2,'y'=4] {'h','l'}, dimensions={0} | all-to-all | bytes 1048576 | tf_op jit(solution)/shard_map/all_to_all | solution.py:168
  275.3 32.1 %reduce-scatter.3.cloned.1.call-done = bf16[512,512]{1,0:T(8,128)(2,1)} async-done(((bf16[4096,512]{1,0:T(8,128)(2,1)}), bf16[512,512]{1,0:T(8,128)(2,1)}) %reduce-scatter.3.cloned.1.call-update) | async-done | bytes 524304 | tf_op jit(solution)/shard_map/reduce_scatter | solution.py:167
  307.4 7.0 %all-to-all-start.9 = ((bf16[8,2,32,512]{3,2,1,0:T(8,128)(2,1)}), bf16[8,2,32,512]{3,2,1,0:T(8,128)(2,1)S(1)}, u32[]{:S(2)}, u32[]{:S(2)}) async-start(bf16[8,2,32,512]{3,2,1,0:T(8,128)(2,1)} %bitcast.36), calls=%async_computation.10 | async-start | bytes 1048576 | tf_op jit(solution)/shard_map/all_to_all | solution.py:168
  314.5 1.1 shard_map.76
  315.5 16.7 %all-to-all-done.9.in_ref = bf16[8,2,32,512]{3,2,1,0:T(8,128)(2,1)S(1)} async-done(((bf16[8,2,32,512]{3,2,1,0:T(8,128)(2,1)}), bf16[8,2,32,512]{3,2,1,0:T(8,128)(2,1)S(1)}, u32[]{:S(2)}, u32[]{:S(2)}) %all-to-all-start.9) | async-done | bytes 524320 | tf_op jit(solution)/shard_map/all_to_all | solution.py:168
  332.2 1.1 shard_map.75
  (23 shorter events, 0.2 us)
Async XLA Ops:
  7.2 10.5 %copy-start.7 = (bf16[512,256]{1,0:T(8,128)(2,1)S(1)}, bf16[512,256]{1,0:T(8,128)(2,1)}, u32[]{:S(2)}) copy-start(bf16[512,256]{1,0:T(8,128)(2,1)} %param.5) | copy-start | bytes 786436
  7.2 14.0 %copy-start.5 = (s32[4,8]{1,0:T(4,128)S(1)}, s32[4,8]{1,0:T(4,128)}, u32[]{:S(2)}) copy-start(s32[4,8]{1,0:T(4,128)} %param.8) | copy-start | bytes 388
  7.2 14.1 %copy-start.6 = (s32[512]{0:T(512)S(1)}, s32[512]{0:T(512)}, u32[]{:S(2)}) copy-start(s32[512]{0:T(512)} %param.9) | copy-start | bytes 6148
  9.2 40.2 %all-to-all-start = ((bf16[8,2,32,512]{3,2,1,0:T(8,128)(2,1)}), bf16[8,2,32,512]{3,2,1,0:T(8,128)(2,1)S(1)}, u32[]{:S(2)}, u32[]{:S(2)}) async-start(bf16[8,2,32,512]{3,2,1,0:T(8,128)(2,1)} %shard_map.68), calls=%async_computation | async-start | bytes 1048576 | tf_op jit(solution)/shard_map/all_to_all | solution.py:160
  17.6 91.8 %all-gather.3.cloned.1.call-start = ((), (), s32[]{:S(2)}) async-start(), calls=%async_computation.13 | async-start | bytes 4718592 | tf_op jit(solution)/shard_map/all_gather | solution.py:163
  17.7 31.7 %collective-permute-start = (bf16[512,256]{1,0:T(8,128)(2,1)S(1)}, bf16[512,256]{1,0:T(8,128)(2,1)S(1)}, u32[]{:S(2)}, u32[]{:S(2)}) collective-permute-start(bf16[512,256]{1,0:T(8,128)(2,1)S(1)} %copy-done.7), channel_id=1, source_target_pairs={{0,0},{1,8},{2,16},{3,24},{8,64},{9,72},{10,80},{11,88},{16,128},{... | collective-permute-start | bytes 786440 | tf_op jit(solution)/shard_map/ppermute | solution.py:181
  21.3 28.1 %collective-permute-start.1 = (s32[544]{0:T(1024)S(1)}, s32[544]{0:T(1024)S(1)}, u32[]{:S(2)}, u32[]{:S(2)}) collective-permute-start(s32[544]{0:T(1024)S(1)} %pad_add_fusion), channel_id=1, source_target_pairs={{0,0},{1,8},{2,16},{3,24},{8,64},{9,72},{10,80},{11,88},{16,128},{... | collective-permute-start | bytes 6536 | tf_op jit(solution)/shard_map/ppermute | solution.py:180
  49.4 0.8 copy-start.4
  50.2 77.4 %all-gather.5.cloned.1.call-start = ((), (), s32[]{:S(2)}) async-start(), calls=%async_computation.14 | async-start | bytes 4718592 | tf_op jit(solution)/shard_map/all_gather | solution.py:163
  80.3 29.2 %all-to-all-start.1 = ((bf16[8,512,128]{2,1,0:T(8,128)(2,1)}), bf16[8,512,128]{2,1,0:T(8,128)(2,1)S(1)}, u32[]{:S(2)}, u32[]{:S(2)}) async-start(bf16[8,512,128]{2,1,0:T(8,128)(2,1)} %bitcast.3), calls=%async_computation.1 | async-start | bytes 2097152 | tf_op jit(solution)/shard_map/all_to_all | solution.py:191
  109.5 2.3 copy-start.1
  122.5 10.6 %all-to-all-start.3 = ((bf16[8,64,256]{2,1,0:T(8,128)(2,1)}), bf16[8,64,256]{2,1,0:T(8,128)(2,1)S(1)}, u32[]{:S(2)}, u32[]{:S(2)}) async-start(bf16[8,64,256]{2,1,0:T(8,128)(2,1)} %broadcast_in_dim.7), calls=%async_computation.3 | async-start | bytes 524288 | tf_op jit(solution)/shard_map/all_to_all | solution.py:128
  136.8 1.3 copy-start.2
  138.1 26.0 %all-to-all-start.5 = ((bf16[4,128,1024]{2,1,0:T(8,128)(2,1)}), bf16[4,128,1024]{2,1,0:T(8,128)(2,1)S(1)}, u32[]{:S(2)}, u32[]{:S(2)}) async-start(bf16[4,128,1024]{2,1,0:T(8,128)(2,1)} %get-tuple-element.16), calls=%async_computation.5 | async-start | bytes 2097152 | tf_op jit(solution)/shard_map/all_to_all | solution.py:207
  141.7 108.9 %reduce-scatter.5.cloned.1.call-start = ((), (), s32[]{:S(2)}) async-start(), calls=%async_computation.16 | async-start | bytes 4718592 | tf_op jit(solution)/shard_map/reduce_scatter | solution.py:167
  164.1 29.8 %copy-start.3 = (bf16[4,256,1024]{2,1,0:T(8,128)(2,1)S(1)}, bf16[4,256,1024]{2,1,0:T(8,128)(2,1)}, u32[]{:S(2)}) copy-start(bf16[4,256,1024]{2,1,0:T(8,128)(2,1)} %copy-done.2) | copy-start | bytes 6291460
  199.0 108.5 %reduce-scatter.3.cloned.1.call-start = ((), (), s32[]{:S(2)}) async-start(), calls=%async_computation.15 | async-start | bytes 4718592 | tf_op jit(solution)/shard_map/reduce_scatter | solution.py:167
  221.8 2.0 copy-start
  307.4 24.8 %all-to-all-start.9 = ((bf16[8,2,32,512]{3,2,1,0:T(8,128)(2,1)}), bf16[8,2,32,512]{3,2,1,0:T(8,128)(2,1)S(1)}, u32[]{:S(2)}, u32[]{:S(2)}) async-start(bf16[8,2,32,512]{3,2,1,0:T(8,128)(2,1)} %bitcast.36), calls=%async_computation.10 | async-start | bytes 1048576 | tf_op jit(solution)/shard_map/all_to_all | solution.py:168
Sparse Core Ops, SparseCore 0:
  50.3 38.6 all-gather.2
  90.9 34.6 all-gather.4
  199.1 51.4 reduce-scatter.4
  252.9 54.4 reduce-scatter.2

commit v6 on v3

--- a/solution.py
+++ b/solution.py
@@ -11,50 +11,81 @@
 
 BLOCK = 128
 VMEM = pltpu.CompilerParams(vmem_limit_bytes=48 * 1024 * 1024)
+MOST_VMEM = pltpu.CompilerParams(vmem_limit_bytes=61 * 1024 * 1024)
 NT = (((1,), (1,)), ((), ()))
 TN = (((0,), (0,)), ((), ()))
 SMEM_SPEC = pl.BlockSpec(memory_space=pltpu.SMEM)
 VMEM_SPEC = pl.BlockSpec(memory_space=pltpu.VMEM)
+HBM_SPEC = pl.BlockSpec(memory_space=pltpu.HBM)
+PIECES = 8
 
 
 def dot(left, right, dims):
     return lax.dot_general(left, right, dims, preferred_element_type=jnp.float32)
 
 
-def pre_kernel(tb, act, ids_ref, tok_ref, enc_ref, out_ref):
+def fetch(tb, act, ids_ref, weight_ref, got_ref, sem):
+    copies = [
+        pltpu.make_async_copy(weight_ref.at[ids_ref[t, a]], got_ref.at[t * act + a], sem.at[t * act + a])
+        for t in range(tb)
+        for a in range(act)
+    ]
+    for copy in copies:
+        copy.start()
+    return lambda pair: copies[pair].wait()
+
+
+def pre_kernel(tb, act, ids_ref, tok_ref, enc_ref, out_ref, got_ref, sem):
+    wait = fetch(tb, act, ids_ref, enc_ref, got_ref, sem)
     for t in range(tb):
         rows = tok_ref[t * BLOCK : (t + 1) * BLOCK, :]
         for a in range(act):
-            out_ref[t * act + a] = dot(rows, enc_ref[ids_ref[t, a]], NT).astype(jnp.bfloat16)
+            pair = t * act + a
+            wait(pair)
+            out_ref[pair] = dot(rows, got_ref[pair], NT).astype(jnp.bfloat16)
 
 
-def sum_rows(tb, act, ids_ref, codes_ref, rows_of, acc_ref, out_ref):
-    acc_ref[...] = jnp.zeros_like(acc_ref)
-    for t in range(tb):
-        rows = rows_of(t)
-        for a in range(act):
-            acc_ref[ids_ref[t, a]] += dot(codes_ref[t * act + a], rows, TN)
-
-    @pl.loop(0, acc_ref.shape[0])
-    def _(b):
-        out_ref[b] = acc_ref[b].astype(jnp.bfloat16)
+def add_rows(t, act, ids_ref, codes_ref, rows, acc_ref):
+    for a in range(act):
+        acc_ref[ids_ref[t, a]] += dot(codes_ref[t * act + a], rows, TN)
 
 
-def dec_kernel(tb, act, ids_ref, tok_ref, weight_ref, codes_ref, dec_ref, part_ref, grad_ref, acc_ref, gout_ref):
+def put(acc_ref, half_ref, out_ref, sem):
+    step = acc_ref.shape[0] // PIECES
+    copies = []
+    for k in range(PIECES):
+        for b in range(k * step, (k + 1) * step):
+            half_ref[b] = acc_ref[b].astype(jnp.bfloat16)
+        here = pl.ds(k * step, step)
+        copies.append(pltpu.make_async_copy(half_ref.at[here], out_ref.at[here], sem.at[k]))
+        copies[-1].start()
+    for copy in copies:
+        copy.wait()
+
+
+def dec_kernel(
+    tb, act, ids_ref, tok_ref, weight_ref, codes_ref, dec_ref, part_ref, grad_ref, acc_ref, half_ref, got_ref, in_sem, out_sem
+):
+    wait = fetch(tb, act, ids_ref, dec_ref, got_ref, in_sem)
+    acc_ref[...] = jnp.zeros_like(acc_ref)
     for t in range(tb):
         here = slice(t * BLOCK, (t + 1) * BLOCK)
         recon = jnp.zeros((BLOCK, tok_ref.shape[1]), jnp.float32)
         for a in range(act):
-            recon += jnp.dot(codes_ref[t * act + a], dec_ref[ids_ref[t, a]], preferred_element_type=jnp.float32)
+            wait(t * act + a)
+            recon += jnp.dot(codes_ref[t * act + a], got_ref[t * act + a], preferred_element_type=jnp.float32)
         gout = (weight_ref[here, :] * (recon - tok_ref[here, :].astype(jnp.float32))).astype(jnp.bfloat16)
-        gout_ref[here, :] = gout
+        add_rows(t, act, ids_ref, codes_ref, gout, acc_ref)
         for a in range(act):
-            part_ref[t * act + a] = dot(gout, dec_ref[ids_ref[t, a]], NT).astype(jnp.bfloat16)
-    sum_rows(tb, act, ids_ref, codes_ref, lambda t: gout_ref[t * BLOCK : (t + 1) * BLOCK, :], acc_ref, grad_ref)
+            part_ref[t * act + a] = dot(gout, got_ref[t * act + a], NT).astype(jnp.bfloat16)
+    put(acc_ref, half_ref, grad_ref, out_sem)
 
 
-def enc_kernel(tb, act, ids_ref, tok_ref, codes_ref, grad_ref, acc_ref):
-    sum_rows(tb, act, ids_ref, codes_ref, lambda t: tok_ref[t * BLOCK : (t + 1) * BLOCK, :], acc_ref, grad_ref)
+def enc_kernel(tb, act, ids_ref, tok_ref, codes_ref, grad_ref, acc_ref, half_ref, out_sem):
+    acc_ref[...] = jnp.zeros_like(acc_ref)
+    for t in range(tb):
+        add_rows(t, act, ids_ref, codes_ref, tok_ref[t * BLOCK : (t + 1) * BLOCK, :], acc_ref)
+    put(acc_ref, half_ref, grad_ref, out_sem)
 
 
 def all_sum(part, axes, n):
@@ -106,22 +137,25 @@
 
     pairs = jax.ShapeDtypeStruct((tb * act, BLOCK, BLOCK), jnp.bfloat16)
     grads = jax.ShapeDtypeStruct((lat_blocks, BLOCK, width), jnp.bfloat16)
-    acc = pltpu.VMEM((lat_blocks, BLOCK, width), jnp.float32)
+    acc = [pltpu.VMEM(grads.shape, jnp.float32), pltpu.VMEM(grads.shape, jnp.bfloat16)]
+    got = pltpu.VMEM((tb * act, BLOCK, width), jnp.bfloat16)
+    in_sem, out_sem = pltpu.SemaphoreType.DMA((tb * act,)), pltpu.SemaphoreType.DMA((PIECES,))
 
     part = pl.pallas_call(
         functools.partial(pre_kernel, tb, act),
         out_shape=pairs,
-        in_specs=[SMEM_SPEC, VMEM_SPEC, VMEM_SPEC],
+        in_specs=[SMEM_SPEC, VMEM_SPEC, HBM_SPEC],
         out_specs=VMEM_SPEC,
-        compiler_params=VMEM,
+        scratch_shapes=[got, in_sem],
+        compiler_params=MOST_VMEM,
     )(ids, tok, enc)
     codes = all_sum(part, feats, nd * ny)
     part, group_dec = pl.pallas_call(
         functools.partial(dec_kernel, tb, act),
         out_shape=(pairs, grads),
-        in_specs=[SMEM_SPEC] + [VMEM_SPEC] * 4,
-        out_specs=(VMEM_SPEC, VMEM_SPEC),
-        scratch_shapes=[acc, pltpu.VMEM((tok_dev, width), jnp.bfloat16)],
+        in_specs=[SMEM_SPEC] + [VMEM_SPEC] * 3 + [HBM_SPEC],
+        out_specs=(VMEM_SPEC, HBM_SPEC),
+        scratch_shapes=acc + [got, in_sem, out_sem],
         compiler_params=VMEM,
     )(ids, tok, weights, codes, dec)
     grad_dec = own_rows(group_dec)
@@ -130,9 +164,9 @@
         functools.partial(enc_kernel, tb, act),
         out_shape=grads,
         in_specs=[SMEM_SPEC] + [VMEM_SPEC] * 2,
-        out_specs=VMEM_SPEC,
-        scratch_shapes=[acc],
-        compiler_params=VMEM,
+        out_specs=HBM_SPEC,
+        scratch_shapes=acc + [out_sem],
+        compiler_params=MOST_VMEM,
     )(ids, tok, grad_codes)
     grad_enc = own_rows(group_enc)
     return (grad_enc, grad_dec)

time: 280 us -> 280 us (level)
  Pallas kernels: 11.3 us -> 21.4 us
  waiting for transfers between devices: 85.7 us -> 78.8 us
  local copies, waits for them, and re-layouts: 8.27 us -> 4.73 us
    all_gather x2, waiting for transfers between devices: 23.7 us -> 16 us  [all_rows(): whole = lax.all_gather(mine, 'z', axis=0, tiled=True)]
    pallas_call x1, Pallas kernels: 1.27 us -> 8.9 us  [per_device(): pl.pallas_call(functools.partial(pre_kernel, tb, act), out_shape=pairs, i...]
    unnamed x10 -> x12, local copies, waits for them, and re-layouts: 4.16 us -> 0.03 us
  transfers between devices with their start and end apart: 8 -> 8, of which waited for: 6 -> 7; matrix products, arithmetic and copies ran while one was open for 2% -> 2% of each run, Pallas kernels for 1% -> 5%
where the time goes in v6:
time: 280 us; the launch traced here: 279 us
  blocking collectives  141 us (50%)
  waiting for transfers between devices  78.8 us (28%)
  Pallas kernels  21.4 us (8%)
  starting transfers between devices  16.2 us (6%)
  between operations  13.9 us (5%)
  local copies, waits for them, and re-layouts  4.73 us (2%)
    reduce_scatter x2, waiting for transfers between devices, own_rows(): lax.psum_scatter(grad.reshape(nz * ny * rows, width), 'z', scatter_dimens...  47.7 us
    all_to_all x2, blocking collectives, all_sum(): got = lax.all_to_all(part, axes, 0, 0, tiled=True)  46.9 us
    all_to_all x2, blocking collectives, per_device(): tok = lax.all_to_all(tok, axes, 0, 0, tiled=True)  34.3 us
    all_to_all x2, blocking collectives, own_features(): got = lax.all_to_all(jnp.stack(quarter), 'y', 0, 0, tiled=True)  25.5 us
    all_to_all x1, blocking collectives, all_sum(): lax.all_to_all(jnp.broadcast_to(mine[None], part.shape), axes, 0, 0, tile...  20.8 us
    all_gather x2, waiting for transfers between devices, all_rows(): whole = lax.all_gather(mine, 'z', axis=0, tiled=True)  16 us
    all_to_all x1, blocking collectives, own_rows(): part = lax.all_to_all(part.reshape(ny, rows, width), 'y', 0, 0, tiled=True)  13.8 us
    pallas_call x1, Pallas kernels, per_device(): pl.pallas_call(functools.partial(pre_kernel, tb, act), out_shape=pairs, i...  8.9 us
  transfers between devices with their start and end apart: 8, of which 7 were waited for; matrix products, arithmetic and copies ran while one was open for 2% of the time, Pallas kernels for 5%

profile of v6, /device:TPU:2, one launch (start us, length us, event | category | flops | bytes accessed | tf_op | source)
XLA Modules:
  0.0 279.0 jit_solution(13253255349863094608)
XLA Ops:
  7.2 0.0 copy-start.3
  7.2 0.0 all-gather.3.cloned.1.call-start
  7.2 1.1 dynamic-slice_bitcast_fusion.7
  8.4 0.0 copy-start.4
  8.4 0.0 copy-start.5
  8.4 0.1 pad_maximum_fusion
  8.5 13.8 %all_to_all.55 = bf16[4,256,256]{2,1,0:T(8,128)(2,1)} all-to-all(bf16[4,256,256]{2,1,0:T(8,128)(2,1)S(1)} %pad_maximum_fusion), channel_id=1, replica_groups=mesh['x'=4,'c'=2,'z'=8,'y'=4] {'y'}, dimensions={0} | all-to-all | bytes 1048576 | tf_op jit(solution)/shard_map/all_to_all | solution.py:117
  22.3 0.0 all-gather.3.cloned.1.call-update
  22.4 0.0 all-gather.5.cloned.1.call-start
  22.4 1.1 dynamic-slice_bitcast_fusion.3
  23.6 0.1 pad_maximum_fusion.1
  23.6 11.7 %all_to_all.56 = bf16[4,256,256]{2,1,0:T(8,128)(2,1)} all-to-all(bf16[4,256,256]{2,1,0:T(8,128)(2,1)S(1)} %pad_maximum_fusion.1), channel_id=1, replica_groups=mesh['x'=4,'c'=2,'z'=8,'y'=4] {'y'}, dimensions={0} | all-to-all | bytes 1048576 | tf_op jit(solution)/shard_map/all_to_all | solution.py:117
  35.3 0.0 all-gather.5.cloned.1.call-update
  35.3 10.7 %all_to_all.57 = bf16[8,64,256]{2,1,0:T(8,128)(2,1)S(1)} all-to-all(bf16[8,64,256]{2,1,0:T(8,128)(2,1)S(1)} %bitcast.54), channel_id=1, replica_groups=mesh['x'=4,'c'=2,'z'=8,'y'=4] {'x','c'}, dimensions={0} | all-to-all | bytes 524288 | tf_op jit(solution)/shard_map/all_to_all | solution.py:135
  46.0 23.6 %all_to_all.58 = bf16[8,64,256]{2,1,0:T(8,128)(2,1)} all-to-all(bf16[8,64,256]{2,1,0:T(8,128)(2,1)S(1)} %all_to_all.57), channel_id=1, replica_groups=mesh['x'=4,'c'=2,'z'=8,'y'=4] {'z'}, dimensions={0} | all-to-all | bytes 524288 | tf_op jit(solution)/shard_map/all_to_all | solution.py:135
  69.6 4.6 %all-to-all-start.3 = ((bf16[8,64,256]{2,1,0:T(8,128)(2,1)}), bf16[8,64,256]{2,1,0:T(8,128)(2,1)S(1)}, u32[]{:S(2)}, u32[]{:S(2)}) async-start(bf16[8,64,256]{2,1,0:T(8,128)(2,1)} %all_to_all.58), calls=%async_computation.3 | async-start | bytes 524288 | tf_op jit(solution)/shard_map/all_to_all | solution.py:135
  74.2 0.1 reshape.51
  74.3 1.9 collective-permute-start
  76.2 5.4 %collective-permute-done = s32[544]{0:T(1024)S(1)} collective-permute-done((s32[544]{0:T(1024)S(1)}, s32[544]{0:T(1024)S(1)}, u32[]{:S(2)}, u32[]{:S(2)}) %collective-permute-start) | collective-permute-done | bytes 2208 | tf_op jit(solution)/shard_map/ppermute | solution.py:109
  81.7 0.7 reshape.52.ids_ref
  82.3 0.0 all-to-all-done.3
  82.4 1.6 all-gather.3.cloned.1.call-done
  83.9 8.9 %shard_map.68 = bf16[32,128,128]{2,1,0:T(8,128)(2,1)} custom-call(s32[4,8]{1,0:T(4,128)} %reshape.52.ids_ref, bf16[512,256]{1,0:T(8,128)(2,1)} %bitcast.43, bf16[64,128,256]{2,1,0:T(8,128)(2,1)} %bitcast.47), custom_call_target="tpu_custom_call" | custom-call | tf_op jit(solution)/shard_map/pallas_call | solution.py:144
  92.8 0.0 copy-start.1
  92.9 25.2 %all_to_all.59 = bf16[32,128,128]{2,1,0:T(8,128)(2,1)S(1)} all-to-all(bf16[32,128,128]{2,1,0:T(8,128)(2,1)} %shard_map.68), channel_id=1, replica_groups=mesh['x'=4,'c'=2,'z'=8,'y'=4] {'x','c','y'}, dimensions={0} | all-to-all | bytes 2097152 | tf_op jit(solution)/shard_map/all_to_all | solution.py:92
  118.0 0.2 reduce_sum.24
  118.2 1.2 broadcast_in_dim.4
  119.4 5.2 %all-to-all-start.5 = ((bf16[32,128,128]{2,1,0:T(8,128)(2,1)}), bf16[32,128,128]{2,1,0:T(8,128)(2,1)S(1)}, u32[]{:S(2)}, u32[]{:S(2)}) async-start(bf16[32,128,128]{2,1,0:T(8,128)(2,1)} %broadcast_in_dim.4), calls=%async_computation.5 | async-start | bytes 2097152 | tf_op jit(solution)/shard_map/all_to_all | solution.py:94
  124.6 0.0 reduce-scatter.5.cloned.1.call-start
  124.7 0.1 copy.7.weight_ref
  124.8 14.4 %all-gather.5.cloned.1.call-done = bf16[8192,256]{1,0:T(8,128)(2,1)} async-done(((bf16[1024,256]{1,0:T(8,128)(2,1)}), bf16[8192,256]{1,0:T(8,128)(2,1)}) %all-gather.5.cloned.1.call-update) | async-done | bytes 4194320 | tf_op jit(solution)/shard_map/all_gather | solution.py:121
  139.2 1.2 all-to-all-done.5.codes_ref
  140.5 7.9 %shard_map.69 = (bf16[32,128,128]{2,1,0:T(8,128)(2,1)S(1)}, bf16[64,128,256]{2,1,0:T(8,128)(2,1)}) custom-call(s32[4,8]{1,0:T(4,128)S(1)} %copy-done.2, bf16[512,256]{1,0:T(8,128)(2,1)S(1)} %bitcast.45, f32[512,1]{1,0:T(8,128)S(1)} %copy.7.weight_ref, bf16[32,128,128]{2,1,0:T(8,128)(2,1)S(1)} %all-to-all-done.5.codes_ref, bf16[64,128,256]{2,1,0:T(8,128)(2,1)} %bitcast.48), custom_call_target="tpu_custom_call" | custom-call | tf_op jit(solution)/shard_map/pallas_call | solution.py:153
  148.3 0.0 reduce-scatter.5.cloned.1.call-update
  148.4 0.0 reduce-scatter.3.cloned.1.call-start
  148.4 21.8 %all_to_all.60 = bf16[32,128,128]{2,1,0:T(8,128)(2,1)S(1)} all-to-all(bf16[32,128,128]{2,1,0:T(8,128)(2,1)S(1)} %get-tuple-element.8), channel_id=1, replica_groups=mesh['x'=4,'c'=2,'z'=8,'y'=4] {'x','c','y'}, dimensions={0} | all-to-all | bytes 2097152 | tf_op jit(solution)/shard_map/all_to_all | solution.py:92
  170.2 0.2 reduce_sum.25
  170.3 0.2 broadcast_in_dim.5
  170.6 20.8 %all_to_all.61.codes_ref = bf16[32,128,128]{2,1,0:T(8,128)(2,1)} all-to-all(bf16[32,128,128]{2,1,0:T(8,128)(2,1)S(1)} %broadcast_in_dim.5), channel_id=1, replica_groups=mesh['x'=4,'c'=2,'z'=8,'y'=4] {'x','c','y'}, dimensions={0} | all-to-all | bytes 2097152 | tf_op jit(solution)/shard_map/all_to_all | solution.py:94
  191.4 4.6 %shard_map.70 = bf16[64,128,256]{2,1,0:T(8,128)(2,1)} custom-call(s32[4,8]{1,0:T(4,128)} %reshape.52.ids_ref, bf16[512,256]{1,0:T(8,128)(2,1)} %bitcast.44, bf16[32,128,128]{2,1,0:T(8,128)(2,1)} %all_to_all.61.codes_ref), custom_call_target="tpu_custom_call" | custom-call | tf_op jit(solution)/shard_map/pallas_call | solution.py:163
  196.0 0.0 reduce-scatter.3.cloned.1.call-update
  196.1 5.1 %reduce-scatter.5.cloned.1.call-done = bf16[1024,256]{1,0:T(8,128)(2,1)} async-done(((bf16[8192,256]{1,0:T(8,128)(2,1)}), bf16[1024,256]{1,0:T(8,128)(2,1)}) %reduce-scatter.5.cloned.1.call-update) | async-done | bytes 524304 | tf_op jit(solution)/shard_map/reduce_scatter | solution.py:125
  201.2 13.8 %all_to_all.62 = bf16[4,256,256]{2,1,0:T(8,128)(2,1)S(1)} all-to-all(bf16[4,256,256]{2,1,0:T(8,128)(2,1)} %bitcast.52), channel_id=1, replica_groups=mesh['x'=4,'c'=2,'z'=8,'y'=4] {'y'}, dimensions={0} | all-to-all | bytes 1048576 | tf_op jit(solution)/shard_map/all_to_all | solution.py:126
  215.0 42.5 %reduce-scatter.3.cloned.1.call-done = bf16[1024,256]{1,0:T(8,128)(2,1)} async-done(((bf16[8192,256]{1,0:T(8,128)(2,1)}), bf16[1024,256]{1,0:T(8,128)(2,1)}) %reduce-scatter.3.cloned.1.call-update) | async-done | bytes 524304 | tf_op jit(solution)/shard_map/reduce_scatter | solution.py:125
  257.6 4.3 %all-to-all-start.9 = ((bf16[4,256,256]{2,1,0:T(8,128)(2,1)}), bf16[4,256,256]{2,1,0:T(8,128)(2,1)S(1)}, u32[]{:S(2)}, u32[]{:S(2)}) async-start(bf16[4,256,256]{2,1,0:T(8,128)(2,1)} %bitcast.53), calls=%async_computation.10 | async-start | bytes 1048576 | tf_op jit(solution)/shard_map/all_to_all | solution.py:126
  261.9 1.1 maximum_convert_fusion.1
  263.0 8.4 %all-to-all-done.9 = bf16[4,256,256]{2,1,0:T(8,128)(2,1)S(1)} async-done(((bf16[4,256,256]{2,1,0:T(8,128)(2,1)}), bf16[4,256,256]{2,1,0:T(8,128)(2,1)S(1)}, u32[]{:S(2)}, u32[]{:S(2)}) %all-to-all-start.9) | async-done | bytes 524320 | tf_op jit(solution)/shard_map/all_to_all | solution.py:126
  271.4 1.1 maximum_convert_fusion
  (13 shorter events, 0.1 us)
Async XLA Ops:
  7.2 28.2 %copy-start.3 = (bf16[512,256]{1,0:T(8,128)(2,1)S(1)}, bf16[512,256]{1,0:T(8,128)(2,1)}, u32[]{:S(2)}) copy-start(bf16[512,256]{1,0:T(8,128)(2,1)} %param.5) | copy-start | bytes 786436
  7.2 76.7 %all-gather.3.cloned.1.call-start = ((), (), s32[]{:S(2)}) async-start(), calls=%async_computation.13 | async-start | bytes 4718592 | tf_op jit(solution)/shard_map/all_gather | solution.py:121
  8.4 65.8 %copy-start.4 = (s32[4,8]{1,0:T(4,128)S(1)}, s32[4,8]{1,0:T(4,128)}, u32[]{:S(2)}) copy-start(s32[4,8]{1,0:T(4,128)} %param.8) | copy-start | bytes 388
  8.4 65.9 %copy-start.5 = (s32[512]{0:T(512)S(1)}, s32[512]{0:T(512)}, u32[]{:S(2)}) copy-start(s32[512]{0:T(512)} %param.9) | copy-start | bytes 6148
  22.4 116.9 %all-gather.5.cloned.1.call-start = ((), (), s32[]{:S(2)}) async-start(), calls=%async_computation.14 | async-start | bytes 4718592 | tf_op jit(solution)/shard_map/all_gather | solution.py:121
  69.6 12.7 %all-to-all-start.3 = ((bf16[8,64,256]{2,1,0:T(8,128)(2,1)}), bf16[8,64,256]{2,1,0:T(8,128)(2,1)S(1)}, u32[]{:S(2)}, u32[]{:S(2)}) async-start(bf16[8,64,256]{2,1,0:T(8,128)(2,1)} %all_to_all.58), calls=%async_computation.3 | async-start | bytes 524288 | tf_op jit(solution)/shard_map/all_to_all | solution.py:135
  74.3 7.4 %collective-permute-start = (s32[544]{0:T(1024)S(1)}, s32[544]{0:T(1024)S(1)}, u32[]{:S(2)}, u32[]{:S(2)}) collective-permute-start(s32[544]{0:T(1024)S(1)} %pad_add_fusion), channel_id=1, source_target_pairs={{0,0},{4,32},{8,64},{12,96},{16,128},{20,160},{24,192},{28,224},{3... | collective-permute-start | bytes 6536 | tf_op jit(solution)/shard_map/ppermute | solution.py:109
  82.4 1.6 copy-start
  92.8 47.6 %copy-start.1 = (bf16[8,64,256]{2,1,0:T(8,128)(2,1)S(1)}, bf16[8,64,256]{2,1,0:T(8,128)(2,1)}, u32[]{:S(2)}) copy-start(bf16[8,64,256]{2,1,0:T(8,128)(2,1)} %copy-done) | copy-start | bytes 786436
  92.8 47.6 %copy-start.2 = (s32[4,8]{1,0:T(4,128)S(1)}, s32[4,8]{1,0:T(4,128)}, u32[]{:S(2)}) copy-start(s32[4,8]{1,0:T(4,128)} %reshape.52.ids_ref) | copy-start | bytes 388
  119.4 21.1 %all-to-all-start.5 = ((bf16[32,128,128]{2,1,0:T(8,128)(2,1)}), bf16[32,128,128]{2,1,0:T(8,128)(2,1)S(1)}, u32[]{:S(2)}, u32[]{:S(2)}) async-start(bf16[32,128,128]{2,1,0:T(8,128)(2,1)} %broadcast_in_dim.4), calls=%async_computation.5 | async-start | bytes 2097152 | tf_op jit(solution)/shard_map/all_to_all | solution.py:94
  124.6 76.6 %reduce-scatter.5.cloned.1.call-start = ((), (), s32[]{:S(2)}) async-start(), calls=%async_computation.16 | async-start | bytes 4718592 | tf_op jit(solution)/shard_map/reduce_scatter | solution.py:125
  148.4 109.2 %reduce-scatter.3.cloned.1.call-start = ((), (), s32[]{:S(2)}) async-start(), calls=%async_computation.15 | async-start | bytes 4718592 | tf_op jit(solution)/shard_map/reduce_scatter | solution.py:125
  257.6 13.8 %all-to-all-start.9 = ((bf16[4,256,256]{2,1,0:T(8,128)(2,1)}), bf16[4,256,256]{2,1,0:T(8,128)(2,1)S(1)}, u32[]{:S(2)}, u32[]{:S(2)}) async-start(bf16[4,256,256]{2,1,0:T(8,128)(2,1)} %bitcast.53), calls=%async_computation.10 | async-start | bytes 1048576 | tf_op jit(solution)/shard_map/all_to_all | solution.py:126
Sparse Core Ops, SparseCore 0:
  22.5 61.4 all-gather.2
  85.7 53.4 all-gather.4
  148.5 52.6 reduce-scatter.4
  203.6 53.9 reduce-scatter.2

commit v7 on v3

--- a/solution.py
+++ b/solution.py
@@ -15,6 +15,8 @@
 TN = (((0,), (0,)), ((), ()))
 SMEM_SPEC = pl.BlockSpec(memory_space=pltpu.SMEM)
 VMEM_SPEC = pl.BlockSpec(memory_space=pltpu.VMEM)
+HBM_SPEC = pl.BlockSpec(memory_space=pltpu.HBM)
+PIECES = 8
 
 
 def dot(left, right, dims):
@@ -40,17 +42,36 @@
         out_ref[b] = acc_ref[b].astype(jnp.bfloat16)
 
 
-def dec_kernel(tb, act, ids_ref, tok_ref, weight_ref, codes_ref, dec_ref, part_ref, grad_ref, acc_ref, gout_ref):
+def put(acc_ref, half_ref, out_ref, sem):
+    step = acc_ref.shape[0] // PIECES
+    copies = []
+    for k in range(PIECES):
+        for b in range(k * step, (k + 1) * step):
+            half_ref[b] = acc_ref[b].astype(jnp.bfloat16)
+        here = pl.ds(k * step, step)
+        copies.append(pltpu.make_async_copy(half_ref.at[here], out_ref.at[here], sem.at[k]))
+        copies[-1].start()
+    for copy in copies:
+        copy.wait()
+
+
+def dec_kernel(
+    tb, act, ids_ref, tok_ref, weight_ref, codes_ref, dec_ref, part_ref, grad_ref, acc_ref, half_ref, got_ref, in_sem, out_sem
+):
+    copy = pltpu.make_async_copy(dec_ref, got_ref, in_sem)
+    copy.start()
+    acc_ref[...] = jnp.zeros_like(acc_ref)
+    copy.wait()
     for t in range(tb):
         here = slice(t * BLOCK, (t + 1) * BLOCK)
         recon = jnp.zeros((BLOCK, tok_ref.shape[1]), jnp.float32)
         for a in range(act):
-            recon += jnp.dot(codes_ref[t * act + a], dec_ref[ids_ref[t, a]], preferred_element_type=jnp.float32)
+            recon += jnp.dot(codes_ref[t * act + a], got_ref[ids_ref[t, a]], preferred_element_type=jnp.float32)
         gout = (weight_ref[here, :] * (recon - tok_ref[here, :].astype(jnp.float32))).astype(jnp.bfloat16)
-        gout_ref[here, :] = gout
         for a in range(act):
-            part_ref[t * act + a] = dot(gout, dec_ref[ids_ref[t, a]], NT).astype(jnp.bfloat16)
-    sum_rows(tb, act, ids_ref, codes_ref, lambda t: gout_ref[t * BLOCK : (t + 1) * BLOCK, :], acc_ref, grad_ref)
+            acc_ref[ids_ref[t, a]] += dot(codes_ref[t * act + a], gout, TN)
+            part_ref[t * act + a] = dot(gout, got_ref[ids_ref[t, a]], NT).astype(jnp.bfloat16)
+    put(acc_ref, half_ref, grad_ref, out_sem)
 
 
 def enc_kernel(tb, act, ids_ref, tok_ref, codes_ref, grad_ref, acc_ref):
@@ -119,9 +140,11 @@
     part, group_dec = pl.pallas_call(
         functools.partial(dec_kernel, tb, act),
         out_shape=(pairs, grads),
-        in_specs=[SMEM_SPEC] + [VMEM_SPEC] * 4,
-        out_specs=(VMEM_SPEC, VMEM_SPEC),
-        scratch_shapes=[acc, pltpu.VMEM((tok_dev, width), jnp.bfloat16)],
+        in_specs=[SMEM_SPEC] + [VMEM_SPEC] * 3 + [HBM_SPEC],
+        out_specs=(VMEM_SPEC, HBM_SPEC),
+        scratch_shapes=[acc]
+        + [pltpu.VMEM(grads.shape, jnp.bfloat16)] * 2
+        + [pltpu.SemaphoreType.DMA, pltpu.SemaphoreType.DMA((PIECES,))],
         compiler_params=VMEM,
     )(ids, tok, weights, codes, dec)
     grad_dec = own_rows(group_dec)

time: 280 us -> 279 us (level)
  no operation moved by 1% of the time
where the time goes in v7:
time: 279 us
  blocking collectives  141 us (51%)
  waiting for transfers between devices  85.7 us (31%)
  starting transfers between devices  16.1 us (6%)
  between operations  13.9 us (5%)
  Pallas kernels  11.1 us (4%)
  local copies, waits for them, and re-layouts  8.27 us (3%)
    reduce_scatter x2, waiting for transfers between devices, own_rows(): lax.psum_scatter(grad.reshape(nz * ny * rows, width), 'z', scatter_dimens...  48.1 us
    all_to_all x2, blocking collectives, all_sum(): got = lax.all_to_all(part, axes, 0, 0, tiled=True)  46.5 us
    all_to_all x2, blocking collectives, per_device(): tok = lax.all_to_all(tok, axes, 0, 0, tiled=True)  34.3 us
    all_to_all x2, blocking collectives, own_features(): got = lax.all_to_all(jnp.stack(quarter), 'y', 0, 0, tiled=True)  25.5 us
    all_gather x2, waiting for transfers between devices, all_rows(): whole = lax.all_gather(mine, 'z', axis=0, tiled=True)  23.7 us
    all_to_all x1, blocking collectives, all_sum(): lax.all_to_all(jnp.broadcast_to(mine[None], part.shape), axes, 0, 0, tile...  20.7 us
    all_to_all x1, blocking collectives, own_rows(): part = lax.all_to_all(part.reshape(ny, rows, width), 'y', 0, 0, tiled=True)  13.8 us
    all_to_all x1, waiting for transfers between devices, own_rows(): part = lax.all_to_all(part.reshape(ny, rows, width), 'y', 0, 0, tiled=True)  8.4 us
  transfers between devices with their start and end apart: 8, of which 6 were waited for; matrix products, arithmetic and copies ran while one was open for 2% of the time, Pallas kernels for 1%

profile of v7, /device:TPU:2, one launch (start us, length us, event | category | flops | bytes accessed | tf_op | source)
XLA Modules:
  0.0 278.6 jit_solution(7118259135657070442)
XLA Ops:
  7.2 0.0 all-gather.3.cloned.1.call-start
  7.2 1.1 dynamic-slice_bitcast_fusion.7
  8.4 0.0 copy-start.3
  8.4 0.0 copy-start.4
  8.4 0.1 pad_maximum_fusion
  8.5 13.8 %all_to_all.55 = bf16[4,256,256]{2,1,0:T(8,128)(2,1)} all-to-all(bf16[4,256,256]{2,1,0:T(8,128)(2,1)S(1)} %pad_maximum_fusion), channel_id=1, replica_groups=mesh['x'=4,'c'=2,'z'=8,'y'=4] {'y'}, dimensions={0} | all-to-all | bytes 1048576 | tf_op jit(solution)/shard_map/all_to_all | solution.py:107
  22.3 0.0 all-gather.3.cloned.1.call-update
  22.4 0.0 all-gather.5.cloned.1.call-start
  22.4 1.1 dynamic-slice_bitcast_fusion.3
  23.6 0.1 pad_maximum_fusion.1
  23.6 11.7 %all_to_all.56 = bf16[4,256,256]{2,1,0:T(8,128)(2,1)} all-to-all(bf16[4,256,256]{2,1,0:T(8,128)(2,1)S(1)} %pad_maximum_fusion.1), channel_id=1, replica_groups=mesh['x'=4,'c'=2,'z'=8,'y'=4] {'y'}, dimensions={0} | all-to-all | bytes 1048576 | tf_op jit(solution)/shard_map/all_to_all | solution.py:107
  35.3 0.0 all-gather.5.cloned.1.call-update
  35.3 10.7 %all_to_all.57 = bf16[8,64,256]{2,1,0:T(8,128)(2,1)S(1)} all-to-all(bf16[8,64,256]{2,1,0:T(8,128)(2,1)S(1)} %bitcast.54), channel_id=1, replica_groups=mesh['x'=4,'c'=2,'z'=8,'y'=4] {'x','c'}, dimensions={0} | all-to-all | bytes 524288 | tf_op jit(solution)/shard_map/all_to_all | solution.py:125
  46.0 23.6 %all_to_all.58 = bf16[8,64,256]{2,1,0:T(8,128)(2,1)} all-to-all(bf16[8,64,256]{2,1,0:T(8,128)(2,1)S(1)} %all_to_all.57), channel_id=1, replica_groups=mesh['x'=4,'c'=2,'z'=8,'y'=4] {'z'}, dimensions={0} | all-to-all | bytes 524288 | tf_op jit(solution)/shard_map/all_to_all | solution.py:125
  69.6 4.6 %all-to-all-start.3 = ((bf16[8,64,256]{2,1,0:T(8,128)(2,1)}), bf16[8,64,256]{2,1,0:T(8,128)(2,1)S(1)}, u32[]{:S(2)}, u32[]{:S(2)}) async-start(bf16[8,64,256]{2,1,0:T(8,128)(2,1)} %all_to_all.58), calls=%async_computation.3 | async-start | bytes 524288 | tf_op jit(solution)/shard_map/all_to_all | solution.py:125
  74.2 0.1 reshape.51
  74.3 1.9 collective-permute-start
  76.2 5.4 %collective-permute-done = s32[544]{0:T(1024)S(1)} collective-permute-done((s32[544]{0:T(1024)S(1)}, s32[544]{0:T(1024)S(1)}, u32[]{:S(2)}, u32[]{:S(2)}) %collective-permute-start) | collective-permute-done | bytes 2208 | tf_op jit(solution)/shard_map/ppermute | solution.py:99
  81.7 0.1 reshape.52.ids_ref
  81.8 0.0 all-to-all-done.3
  81.8 2.2 all-gather.3.cloned.1.call-done
  83.9 2.2 copy-done.1
  86.1 1.3 shard_map.68
  87.4 23.5 %all_to_all.59 = bf16[32,128,128]{2,1,0:T(8,128)(2,1)S(1)} all-to-all(bf16[32,128,128]{2,1,0:T(8,128)(2,1)S(1)} %shard_map.68), channel_id=1, replica_groups=mesh['x'=4,'c'=2,'z'=8,'y'=4] {'x','c','y'}, dimensions={0} | all-to-all | bytes 2097152 | tf_op jit(solution)/shard_map/all_to_all | solution.py:82
  110.9 0.2 reduce_sum.24
  111.1 1.2 broadcast_in_dim.4
  112.3 5.2 %all-to-all-start.5 = ((bf16[32,128,128]{2,1,0:T(8,128)(2,1)}), bf16[32,128,128]{2,1,0:T(8,128)(2,1)S(1)}, u32[]{:S(2)}, u32[]{:S(2)}) async-start(bf16[32,128,128]{2,1,0:T(8,128)(2,1)} %broadcast_in_dim.4), calls=%async_computation.5 | async-start | bytes 2097152 | tf_op jit(solution)/shard_map/all_to_all | solution.py:84
  117.5 0.0 reduce-scatter.5.cloned.1.call-start
  117.6 0.1 copy.7.weight_ref
  117.7 21.5 %all-gather.5.cloned.1.call-done = bf16[8192,256]{1,0:T(8,128)(2,1)} async-done(((bf16[1024,256]{1,0:T(8,128)(2,1)}), bf16[8192,256]{1,0:T(8,128)(2,1)}) %all-gather.5.cloned.1.call-update) | async-done | bytes 4194320 | tf_op jit(solution)/shard_map/all_gather | solution.py:111
  139.2 0.0 all-to-all-done.5.codes_ref
  139.2 7.4 %shard_map.69 = (bf16[32,128,128]{2,1,0:T(8,128)(2,1)S(1)}, bf16[64,128,256]{2,1,0:T(8,128)(2,1)}) custom-call(s32[4,8]{1,0:T(4,128)S(1)} %reshape.52.ids_ref, bf16[512,256]{1,0:T(8,128)(2,1)S(1)} %bitcast.46, f32[512,1]{1,0:T(8,128)S(1)} %copy.7.weight_ref, bf16[32,128,128]{2,1,0:T(8,128)(2,1)S(1)} %all-to-all-done.5.codes_ref, bf16[64,128,256]{2,1,0:T(8,128)(2,1)} %bitcast.48), custom_call_target="tpu_custom_call" | custom-call | tf_op jit(solution)/shard_map/pallas_call | solution.py:140
  146.7 0.0 reduce-scatter.5.cloned.1.call-update
  146.7 0.0 reduce-scatter.3.cloned.1.call-start
  146.7 23.0 %all_to_all.60 = bf16[32,128,128]{2,1,0:T(8,128)(2,1)S(1)} all-to-all(bf16[32,128,128]{2,1,0:T(8,128)(2,1)S(1)} %get-tuple-element.8), channel_id=1, replica_groups=mesh['x'=4,'c'=2,'z'=8,'y'=4] {'x','c','y'}, dimensions={0} | all-to-all | bytes 2097152 | tf_op jit(solution)/shard_map/all_to_all | solution.py:82
  169.7 0.2 reduce_sum.25
  169.9 0.2 broadcast_in_dim.5
  170.1 20.7 %all_to_all.61.codes_ref = bf16[32,128,128]{2,1,0:T(8,128)(2,1)S(1)} all-to-all(bf16[32,128,128]{2,1,0:T(8,128)(2,1)S(1)} %broadcast_in_dim.5), channel_id=1, replica_groups=mesh['x'=4,'c'=2,'z'=8,'y'=4] {'x','c','y'}, dimensions={0} | all-to-all | bytes 2097152 | tf_op jit(solution)/shard_map/all_to_all | solution.py:84
  190.8 2.4 shard_map.70
  193.2 2.0 copy-done
  195.2 0.0 reduce-scatter.3.cloned.1.call-update
  195.2 5.6 %reduce-scatter.5.cloned.1.call-done = bf16[1024,256]{1,0:T(8,128)(2,1)} async-done(((bf16[8192,256]{1,0:T(8,128)(2,1)}), bf16[1024,256]{1,0:T(8,128)(2,1)}) %reduce-scatter.5.cloned.1.call-update) | async-done | bytes 524304 | tf_op jit(solution)/shard_map/reduce_scatter | solution.py:115
  200.8 13.8 %all_to_all.62 = bf16[4,256,256]{2,1,0:T(8,128)(2,1)S(1)} all-to-all(bf16[4,256,256]{2,1,0:T(8,128)(2,1)} %bitcast.52), channel_id=1, replica_groups=mesh['x'=4,'c'=2,'z'=8,'y'=4] {'y'}, dimensions={0} | all-to-all | bytes 1048576 | tf_op jit(solution)/shard_map/all_to_all | solution.py:116
  214.6 42.6 %reduce-scatter.3.cloned.1.call-done = bf16[1024,256]{1,0:T(8,128)(2,1)} async-done(((bf16[8192,256]{1,0:T(8,128)(2,1)}), bf16[1024,256]{1,0:T(8,128)(2,1)}) %reduce-scatter.3.cloned.1.call-update) | async-done | bytes 524304 | tf_op jit(solution)/shard_map/reduce_scatter | solution.py:115
  257.1 4.3 %all-to-all-start.9 = ((bf16[4,256,256]{2,1,0:T(8,128)(2,1)}), bf16[4,256,256]{2,1,0:T(8,128)(2,1)S(1)}, u32[]{:S(2)}, u32[]{:S(2)}) async-start(bf16[4,256,256]{2,1,0:T(8,128)(2,1)} %bitcast.53), calls=%async_computation.10 | async-start | bytes 1048576 | tf_op jit(solution)/shard_map/all_to_all | solution.py:116
  261.4 1.1 maximum_convert_fusion.1
  262.5 8.4 %all-to-all-done.9 = bf16[4,256,256]{2,1,0:T(8,128)(2,1)S(1)} async-done(((bf16[4,256,256]{2,1,0:T(8,128)(2,1)}), bf16[4,256,256]{2,1,0:T(8,128)(2,1)S(1)}, u32[]{:S(2)}, u32[]{:S(2)}) %all-to-all-start.9) | async-done | bytes 524320 | tf_op jit(solution)/shard_map/all_to_all | solution.py:116
  271.0 1.1 maximum_convert_fusion
  (11 shorter events, 0.1 us)
Async XLA Ops:
  7.2 28.2 %copy-start.2 = (bf16[512,256]{1,0:T(8,128)(2,1)S(1)}, bf16[512,256]{1,0:T(8,128)(2,1)}, u32[]{:S(2)}) copy-start(bf16[512,256]{1,0:T(8,128)(2,1)} %param.5) | copy-start | bytes 786436
  7.2 76.7 %all-gather.3.cloned.1.call-start = ((), (), s32[]{:S(2)}) async-start(), calls=%async_computation.13 | async-start | bytes 4718592 | tf_op jit(solution)/shard_map/all_gather | solution.py:111
  8.4 65.8 %copy-start.3 = (s32[4,8]{1,0:T(4,128)S(1)}, s32[4,8]{1,0:T(4,128)}, u32[]{:S(2)}) copy-start(s32[4,8]{1,0:T(4,128)} %param.8) | copy-start | bytes 388
  8.4 65.9 %copy-start.4 = (s32[512]{0:T(512)S(1)}, s32[512]{0:T(512)}, u32[]{:S(2)}) copy-start(s32[512]{0:T(512)} %param.9) | copy-start | bytes 6148
  22.4 116.9 %all-gather.5.cloned.1.call-start = ((), (), s32[]{:S(2)}) async-start(), calls=%async_computation.14 | async-start | bytes 4718592 | tf_op jit(solution)/shard_map/all_gather | solution.py:111
  69.6 12.1 %all-to-all-start.3 = ((bf16[8,64,256]{2,1,0:T(8,128)(2,1)}), bf16[8,64,256]{2,1,0:T(8,128)(2,1)S(1)}, u32[]{:S(2)}, u32[]{:S(2)}) async-start(bf16[8,64,256]{2,1,0:T(8,128)(2,1)} %all_to_all.58), calls=%async_computation.3 | async-start | bytes 524288 | tf_op jit(solution)/shard_map/all_to_all | solution.py:125
  74.3 7.4 %collective-permute-start = (s32[544]{0:T(1024)S(1)}, s32[544]{0:T(1024)S(1)}, u32[]{:S(2)}, u32[]{:S(2)}) collective-permute-start(s32[544]{0:T(1024)S(1)} %pad_add_fusion), channel_id=1, source_target_pairs={{0,0},{4,32},{8,64},{12,96},{16,128},{20,160},{24,192},{28,224},{3... | collective-permute-start | bytes 6536 | tf_op jit(solution)/shard_map/ppermute | solution.py:99
  83.9 2.2 copy-start.1
  112.3 26.9 %all-to-all-start.5 = ((bf16[32,128,128]{2,1,0:T(8,128)(2,1)}), bf16[32,128,128]{2,1,0:T(8,128)(2,1)S(1)}, u32[]{:S(2)}, u32[]{:S(2)}) async-start(bf16[32,128,128]{2,1,0:T(8,128)(2,1)} %broadcast_in_dim.4), calls=%async_computation.5 | async-start | bytes 2097152 | tf_op jit(solution)/shard_map/all_to_all | solution.py:84
  117.5 83.2 %reduce-scatter.5.cloned.1.call-start = ((), (), s32[]{:S(2)}) async-start(), calls=%async_computation.16 | async-start | bytes 4718592 | tf_op jit(solution)/shard_map/reduce_scatter | solution.py:115
  146.7 110.4 %reduce-scatter.3.cloned.1.call-start = ((), (), s32[]{:S(2)}) async-start(), calls=%async_computation.15 | async-start | bytes 4718592 | tf_op jit(solution)/shard_map/reduce_scatter | solution.py:115
  193.2 2.0 copy-start
  257.1 13.8 %all-to-all-start.9 = ((bf16[4,256,256]{2,1,0:T(8,128)(2,1)}), bf16[4,256,256]{2,1,0:T(8,128)(2,1)S(1)}, u32[]{:S(2)}, u32[]{:S(2)}) async-start(bf16[4,256,256]{2,1,0:T(8,128)(2,1)} %bitcast.53), calls=%async_computation.10 | async-start | bytes 1048576 | tf_op jit(solution)/shard_map/all_to_all | solution.py:116
Sparse Core Ops, SparseCore 0:
  22.5 61.4 all-gather.2
  85.7 53.4 all-gather.4
  146.8 53.8 reduce-scatter.4
  203.2 53.9 reduce-scatter.2
